TPU v7x, 32 devices: a whole 2x2x4 slice. The times are simulated.
32 devices in a mesh: dp: 16 (over z, y, x), rows: 2 (over core).
Axes of the slice: x: 2, y: 2, z: 4, core: 2. Of those that a mesh axis runs over, the one named last changes fastest.
Arguments:
- glob_in: bfloat16 [16, 28, 28, 1492], P('dp', 'rows'), may hold values from -6 to 6
- small_in: bfloat16 [80, 12, 12, 1492], P('dp', 'rows'), may hold values from -6 to 6
- small_count: int32 [16], P('dp'), may hold values from 1 to 5, as said below
- kernel_in: bfloat16 [1492, 1492], P(None, 'rows'), may hold values from -0.15625 to 0.15625
- kernel_mid: bfloat16 [3, 3, 373, 1492], P(None, None, None, 'rows'), may hold values from -0.109375 to 0.109375
- kernel_out: bfloat16 [1492, 1492], P(None, 'rows'), may hold values from -0.15625 to 0.15625
- squeeze_weight: bfloat16 [1492, 373], P('rows'), may hold values from -0.3125 to 0.3125
- squeeze_bias: bfloat16 [373], replicated, may hold values from -3 to 3
- excite_weight: bfloat16 [373, 1492], P(None, 'rows'), may hold values from -0.625 to 0.625
- excite_bias: bfloat16 [1492], P('rows'), may hold values from -3 to 3
- gain_first: bfloat16 [1492], P('rows'), may hold values from 0.099609375 to 1.8984375
- shift_first: bfloat16 [1492], P('rows'), may hold values from -3 to 3
- gain_second: bfloat16 [1492], P('rows'), may hold values from 0.099609375 to 1.8984375
- shift_second: bfloat16 [1492], P('rows'), may hold values from -3 to 3
- gain_third: bfloat16 [1492], P('rows'), may hold values from 0.099609375 to 1.8984375
- shift_third: bfloat16 [1492], P('rows'), may hold values from -3 to 3
- glob_cotangent: bfloat16 [16, 28, 28, 1492], P('dp', 'rows'), may hold values from -6 to 6
- small_cotangent: bfloat16 [80, 12, 12, 1492], P('dp', 'rows'), may hold values from -6 to 6
Outputs:
- glob_out: float32 [16, 28, 28, 1492], P('dp', 'rows')
- small_out: float32 [80, 12, 12, 1492], P('dp', 'rows')
- glob_grad: float32 [16, 28, 28, 1492], P('dp', 'rows')
- small_grad: float32 [80, 12, 12, 1492], P('dp', 'rows')
- grad_kernel_in: float32 [1492, 1492], P(None, 'rows')
- grad_kernel_mid: float32 [3, 3, 373, 1492], P(None, None, None, 'rows')
- grad_kernel_out: float32 [1492, 1492], P(None, 'rows')
- grad_squeeze_weight: float32 [1492, 373], P('rows')
- grad_squeeze_bias: float32 [373], replicated
- grad_excite_weight: float32 [373, 1492], P(None, 'rows')
- grad_excite_bias: float32 [1492], P('rows')
- grad_gain_first: float32 [1492], P('rows')
- grad_shift_first: float32 [1492], P('rows')
- grad_gain_second: float32 [1492], P('rows')
- grad_shift_second: float32 [1492], P('rows')
- grad_gain_third: float32 [1492], P('rows')
- grad_shift_third: float32 [1492], P('rows')
Inputs may be any that keep to these rules, and one draw needn't show every extreme that they name: Block b's live small crops are its first small_count[b] slots; some block uses all 5.
All inputs are finite; a program needn't handle non-finite values.
Results may differ from a plain program's by a relative error of at most 0.017.
Values may be sent and summed in bfloat16 or wider, within the bound.
A program may use at most 384 MiB of HBM per device.

v0:
```python
import functools

import jax
import jax.numpy as jnp
from jax import lax
from jax.experimental import pallas as pl
from jax.experimental.pallas import tpu as pltpu
from jax.sharding import PartitionSpec as P

EPSILON = 1e-05
MESH = pl.DeviceIdType.MESH
F32 = jnp.float32
BF16 = jnp.bfloat16
ANY = pl.BlockSpec(memory_space=pl.ANY)
VMEM = pl.BlockSpec(memory_space=pltpu.VMEM)
LANE = 128
TILE = 64
VMEM_BYTES = 62 * 1024 * 1024


def round_up(value, step):
    return -(-value // step) * step


class Plan:
    def __init__(self, glob_shape, small_shape, group_width, dp):
        self.glob_height, self.glob_side = glob_shape[1], glob_shape[2]
        self.slots, self.small_height, self.small_side = small_shape[:3]
        self.channels = glob_shape[3]
        self.glob_width = round_up(self.glob_side + 1, 32)
        self.small_width = round_up(self.small_side + 1, 16)
        self.glob_own = self.glob_height * self.glob_width
        self.slot_own = self.small_height * self.small_width
        self.own = self.glob_own + self.slots * self.slot_own
        self.glob_all = 2 * self.glob_own
        self.slot_all = 2 * self.slot_own
        self.all = 2 * self.own
        self.glob_base = self.glob_width
        self.small_base = self.glob_all + 2 * self.glob_width
        self.slot_conv = self.slot_all + self.small_width
        self.small_conv = self.slots * self.slot_conv
        self.conv = self.small_base + self.small_conv
        self.width = group_width
        self.group = round_up(group_width, LANE)
        self.half = 2 * self.group
        self.half_real = self.channels // 2
        self.dp = dp
        self.glob_tiles = self.glob_all // TILE
        self.slot_tiles = self.slot_all // TILE
        self.slot_rows = round_up(1 + self.slots, 8)
        self.glob_area = float(2 * self.glob_height * self.glob_side)
        self.slot_area = float(2 * self.small_height * self.small_side)

    def own_pieces(self, core):
        pieces = [(pl.multiple_of(core * self.glob_own, 16), 0, self.glob_own)]
        for slot in range(self.slots):
            place = self.glob_all + slot * self.slot_all + core * self.slot_own
            pieces.append(
                (pl.multiple_of(place, 16), self.glob_own + slot * self.slot_own, self.slot_own)
            )
        return pieces

    def sweep(self, body, carry):
        def glob_step(tile, state):
            start = pl.multiple_of(tile * TILE, TILE)
            return body(start, pl.multiple_of(self.glob_base + start, 16), 0, state)

        def slot_step(tile, state):
            slot = tile // self.slot_tiles
            start = pl.multiple_of(self.glob_all + tile * TILE, TILE)
            place = self.small_base + tile * TILE + slot * self.small_width
            return body(start, pl.multiple_of(place, 16), 1 + slot, state)

        carry = lax.fori_loop(0, self.glob_tiles, glob_step, carry)
        return lax.fori_loop(0, self.slots * self.slot_tiles, slot_step, carry)

    def segments(self):
        return (
            (self.glob_base, self.glob_all, self.glob_width),
            (self.small_base, self.small_conv - self.small_width, self.small_width),
        )


def sigmoid(value):
    return 0.5 * jnp.tanh(0.5 * value) + 0.5


def rows_down(tile):
    return jnp.sum(tile.reshape(tile.shape[0] // 8, 8, tile.shape[1]), 0)


def widen(mask, lanes):
    return jnp.concatenate([mask] * (lanes // mask.shape[1]), 1)


def dot(left, right):
    return jnp.dot(left, right, preferred_element_type=F32)


def dot_nt(left, right):
    return lax.dot_general(left, right, (((1,), (1,)), ((), ())), preferred_element_type=F32)


def dot_tn(left, right):
    return lax.dot_general(left, right, (((0,), (0,)), ((), ())), preferred_element_type=F32)


def split_dot(left, right, nt=False):
    high = left.astype(BF16)
    low = (left - high.astype(F32)).astype(BF16)
    call = dot_nt if nt else dot
    return call(high, right) + call(low, right)


def entry_barrier(n, me, core):
    barrier = pltpu.get_barrier_semaphore()

    def greet(step, carry):
        pl.semaphore_signal(
            barrier, inc=1, device_id=(lax.rem(me + step, n), core), device_id_type=MESH
        )
        return carry

    lax.fori_loop(1, n, greet, 0)
    pl.semaphore_signal(barrier, inc=1, device_id=(me, 1 - core), device_id_type=MESH)
    pl.semaphore_wait(barrier, n)


class Spread:
    def __init__(self, n, me, core, source, slots, send, recv):
        self.n, self.me, self.core = n, me, core
        self.source, self.slots, self.send, self.recv = source, slots, send, recv

    def copy(self, step):
        return pltpu.make_async_remote_copy(
            src_ref=self.source,
            dst_ref=self.slots.at[self.me],
            send_sem=self.send.at[step],
            recv_sem=self.recv.at[step],
            device_id=(lax.rem(self.me + step, self.n), self.core),
            device_id_type=MESH,
        )

    def start(self):
        def begin(step, carry):
            self.copy(step).start()
            return carry

        lax.fori_loop(1, self.n, begin, 0)
        self.slots[pl.ds(self.me, 1)] = self.source[...][None]

    def wait(self):
        def end(step, carry):
            self.copy(step).wait()
            return carry

        lax.fori_loop(1, self.n, end, 0)


def to_partner(me, core, source, target, send, recv):
    return pltpu.make_async_remote_copy(
        src_ref=source,
        dst_ref=target,
        send_sem=send,
        recv_sem=recv,
        device_id=(me, 1 - core),
        device_id_type=MESH,
    )


def merge_moments(slots, n, lanes):
    def add(step, carry):
        total, count = carry
        return (total + slots[step, :, :lanes], count + slots[step, :, 2 * lanes : 2 * lanes + LANE])

    total, count = lax.fori_loop(
        0, n, add, (jnp.zeros((1, lanes), F32), jnp.zeros((1, LANE), F32))
    )
    wide_count = widen(count, lanes)
    mean = total / wide_count

    def spread(step, carry):
        own_count = widen(slots[step, :, 2 * lanes : 2 * lanes + LANE], lanes)
        gap = slots[step, :, :lanes] / own_count - mean
        return carry + slots[step, :, lanes : 2 * lanes] + own_count * gap * gap

    squares = lax.fori_loop(0, n, spread, jnp.zeros((1, lanes), F32))
    return mean, squares / wide_count, wide_count


def local_moments(plan, values, mask, which, count):
    lanes = plan.half

    def add(start, place, crop, carry):
        row = start if which == "all" else place
        tile = values[pl.ds(row, TILE), :] * widen(mask[pl.ds(start, TILE), :], lanes)
        return carry + rows_down(tile)

    total = jnp.sum(plan.sweep(add, jnp.zeros((8, lanes), F32)), 0, keepdims=True)
    mean = total / count

    def spread(start, place, crop, carry):
        row = start if which == "all" else place
        gap = (values[pl.ds(row, TILE), :] - mean) * widen(mask[pl.ds(start, TILE), :], lanes)
        return carry + rows_down(gap * gap)

    squares = jnp.sum(plan.sweep(spread, jnp.zeros((8, lanes), F32)), 0, keepdims=True)
    return total, squares


GAIN_ONE, SHIFT_ONE, GAIN_TWO, SHIFT_TWO, EXCITE_BIAS, SQUEEZE_BIAS, COUNT = range(7)
MEAN_ONE, INVERSE_ONE, MEAN_TWO, INVERSE_TWO, TOTAL = range(5)


def lane_of(shape):
    return lax.broadcasted_iota(jnp.int32, shape, len(shape) - 1)


def row_of(shape):
    return lax.broadcasted_iota(jnp.int32, shape, len(shape) - 2)


def group_lanes(value, plan):
    lane = lane_of(value.shape)
    moved = pltpu.roll(value, plan.group - plan.width, 1)
    return jnp.where(lane < plan.width, value, jnp.where(lane < plan.group, 0.0, moved))


def fill_mask(plan, mask, crops, slot_rows, live_count):
    step = 32
    row = row_of((step, LANE))
    glob = (lax.rem(row, plan.glob_width) < plan.glob_side).astype(F32)
    small = (lax.rem(row, plan.small_width) < plan.small_side).astype(F32)

    def glob_step(tile, carry):
        mask[pl.ds(pl.multiple_of(tile * step, step), step), :] = glob
        return carry

    lax.fori_loop(0, crops // step, glob_step, 0)
    for slot in range(plan.slots):
        live = jnp.clip(live_count - float(slot), 0.0, 1.0)

        def slot_step(tile, carry, slot=slot, live=live):
            start = crops + slot * slot_rows + tile * step
            mask[pl.ds(pl.multiple_of(start, step), step), :] = small * live
            return carry

        lax.fori_loop(0, slot_rows // step, slot_step, 0)


def zero_borders(plan, shifted):
    lanes = shifted.shape[2]
    for side in range(2):
        shifted[side, : plan.glob_base, :] = jnp.zeros((plan.glob_base, lanes), BF16)
        shifted[side, plan.glob_base + plan.glob_all : plan.small_base, :] = jnp.zeros(
            (plan.glob_width, lanes), BF16
        )
        for slot in range(plan.slots):
            low = plan.small_base + slot * plan.slot_conv + plan.slot_all
            shifted[side, low : low + plan.small_width, :] = jnp.zeros(
                (plan.small_width, lanes), BF16
            )


def forward_kernel(
    plan,
    live,
    glob_hbm,
    small_hbm,
    kernel_in_hbm,
    kernel_mid_hbm,
    kernel_out_hbm,
    squeeze_hbm,
    excite_hbm,
    vec_raw,
    x_out,
    pre_one_out,
    act_one_out,
    pre_two_out,
    act_three_out,
    w_mid_out,
    k_out_both,
    w_in_both,
    vec_three_other,
    vec,
    mask,
    w_squeeze,
    w_excite,
    stats,
    pooled_out,
    excite_out,
    squeeze_pre_out,
    glob,
    small,
    kernel_in,
    taps,
    kernel_out,
    squeeze,
    excite,
    wide,
    table,
    x_all,
    pre_one,
    shifted,
    w_in,
    w_mid,
    pre_two,
    act_three,
    k_out,
    pay_one,
    slots_one,
    pay_two,
    slots_two,
    squeeze_send,
    squeeze_recv,
    local_sem,
    send_sem,
    recv_sem,
    spread_send,
    spread_recv,
):
    n, half, group, width = plan.dp, plan.half, plan.group, plan.width
    channels, real = plan.channels, plan.half_real
    me, core = lax.axis_index("dp"), lax.axis_index("rows")
    pieces = plan.own_pieces(core)

    def local(source, target, index):
        copy = pltpu.make_async_copy(source, target, local_sem.at[index])
        copy.start()
        return copy

    load_glob = local(glob_hbm, glob, 0)
    load_small = local(small_hbm, small, 1)
    load_in = local(kernel_in_hbm, kernel_in, 2)
    load_taps = [local(kernel_mid_hbm.at[tap], taps.at[tap], 3 + tap) for tap in range(3)]
    load_out = local(kernel_out_hbm, kernel_out, 6)
    load_squeeze = local(squeeze_hbm, squeeze, 7)
    load_excite = local(excite_hbm, excite, 8)
    entry_barrier(n, me, core)

    def partner(source, target, index):
        copy = to_partner(me, core, source, target, send_sem.at[index], recv_sem.at[index])
        copy.start()
        return copy

    load_glob.wait()

    def glob_row(row, carry):
        start = pieces[0][0] + row * plan.glob_width
        rows = pl.ds(pl.multiple_of(start, 16), plan.glob_width)
        wide[: plan.glob_side, :channels] = glob[row].astype(F32)
        for side in range(2):
            x_all[side, rows, :] = wide[: plan.glob_width, side * half : (side + 1) * half].astype(BF16)
        return carry

    def small_row(row, carry):
        slot = row // plan.small_height
        start = plan.glob_all + slot * plan.slot_all + core * plan.slot_own
        start = start + lax.rem(row, plan.small_height) * plan.small_width
        rows = pl.ds(pl.multiple_of(start, 16), plan.small_width)
        wide[: plan.small_side, :channels] = small[row].astype(F32)
        for side in range(2):
            x_all[side, rows, :] = wide[: plan.small_width, side * half : (side + 1) * half].astype(
                BF16
            )
        return carry

    def send_piece(index):
        part = x_all.at[:, pl.ds(pieces[index][0], pieces[index][2]), :]
        return partner(part, part, index)

    wide[...] = jnp.zeros_like(wide)
    lax.fori_loop(0, plan.glob_height, glob_row, 0)
    x_remote = [send_piece(0)]
    load_small.wait()
    wide[...] = jnp.zeros_like(wide)
    lax.fori_loop(0, plan.slots * plan.small_height, small_row, 0)
    x_remote += [send_piece(1 + slot) for slot in range(plan.slots)]

    table[...] = jnp.zeros_like(table)
    load_in.wait()
    for start in range(0, channels, group):
        length = min(group, channels - start)
        table[:length, :real] = kernel_in[start : start + length, :].astype(F32)
        block = group_lanes(table[:group, :], plan)
        if length < group:
            block = jnp.where(row_of(block.shape) < length, block, 0.0)
        low = start % half
        w_in[start // half, low : low + group, :] = block.astype(BF16)
    base = len(pieces)
    send_in = partner(w_in, w_in_both.at[core], base)

    live_count = live[0].astype(F32)
    raw = vec_raw[:8, :]
    grouped = group_lanes(raw, plan)
    chip_count = jnp.zeros((1, half), F32) + (plan.glob_area + plan.slot_area * live_count)
    row = row_of(raw.shape)
    vec[...] = jnp.where(row == SQUEEZE_BIAS, raw, jnp.where(row == COUNT, chip_count, grouped))
    send_vec = partner(vec_raw.at[pl.ds(8, 8), :], vec_three_other, base + 1)
    fill_mask(plan, mask, plan.glob_all, plan.slot_all, live_count)

    def product(owner):
        place = pl.multiple_of(owner * plan.glob_own, 16)
        rows = pl.ds(place, plan.glob_own)
        pre_one[rows, :] = dot(x_all[0, rows, :], w_in[0]) + dot(x_all[1, rows, :], w_in[1])
        places = [spot for spot, _, _ in plan.own_pieces(owner)[1:]]
        sides = [
            jnp.concatenate([x_all[side, pl.ds(spot, plan.slot_own), :] for spot in places], 0)
            for side in range(2)
        ]
        result = dot(sides[0], w_in[0]) + dot(sides[1], w_in[1])
        for slot, spot in enumerate(places):
            pre_one[pl.ds(spot, plan.slot_own), :] = result[
                slot * plan.slot_own : (slot + 1) * plan.slot_own
            ]

    def prepare_tap(tap):
        load_taps[tap].wait()
        table[:width, :real] = taps[tap % 3].astype(F32)
        block = group_lanes(table[:group, :], plan)
        block = jnp.where(row_of(block.shape) < width, block, 0.0)
        w_mid[tap // 3, tap % 3 * group : (tap % 3 + 1) * group, :] = block.astype(BF16)
        if tap + 3 < 9:
            load_taps.append(local(kernel_mid_hbm.at[tap + 3], taps.at[tap % 3], 3 + tap % 3))

    product(core)
    zero_borders(plan, shifted)
    for copy in x_remote:
        copy.wait()
    product(1 - core)
    saves = [local(x_all, x_out, 9), local(pre_one, pre_one_out, 10)]

    def local_part(values, which, pay):
        total, squares = local_moments(plan, values, mask, which, vec[COUNT : COUNT + 1, :])
        pay[:, :half] = total
        pay[:, half : 2 * half] = squares
        pay[:, 2 * half :] = vec[COUNT : COUNT + 1, :LANE]

    def spread_of(pay, slots, index):
        spread = Spread(n, me, core, pay, slots, spread_send.at[index], spread_recv.at[index])
        spread.start()
        return spread

    local_part(pre_one, "all", pay_one)
    spread = spread_of(pay_one, slots_one, 0)
    for tap in range(9):
        prepare_tap(tap)
    saves.append(local(w_mid, w_mid_out, 11))
    spread.wait()
    mean, variance, count = merge_moments(slots_one, n, half)
    inverse = lax.rsqrt(variance + EPSILON)
    stats[...] = jnp.zeros_like(stats)
    stats[MEAN_ONE : MEAN_ONE + 1, :] = mean
    stats[INVERSE_ONE : INVERSE_ONE + 1, :] = inverse
    stats[TOTAL : TOTAL + 1, :] = count
    scale = inverse * vec[GAIN_ONE : GAIN_ONE + 1, :]
    shift = vec[SHIFT_ONE : SHIFT_ONE + 1, :]

    def activate_one(start, place, crop, carry):
        norm = (pre_one[pl.ds(start, TILE), :] - mean) * scale + shift
        act = norm * sigmoid(norm) * widen(mask[pl.ds(start, TILE), :], half)
        before = pltpu.roll(act, 1, 0)
        after = pltpu.roll(act, TILE - 1, 0)
        for tap, value in enumerate((before, act, after)):
            for side in range(2):
                shifted[side, pl.ds(place, TILE), tap * group : (tap + 1) * group] = value[
                    :, side * group : (side + 1) * group
                ].astype(BF16)
        return carry

    plan.sweep(activate_one, 0)
    for side in range(2):
        saves.append(
            local(
                shifted.at[side, :, group : 2 * group],
                act_one_out.at[:, side * group : (side + 1) * group],
                12 + side,
            )
        )

    for low, length, wide_row in plan.segments():
        for side in range(2):
            lanes = slice(side * group, (side + 1) * group)
            block = length // 2
            for part in range(2):
                at = low + part * block
                total = None
                for tap in range(3):
                    first = at + (tap - 1) * wide_row
                    term = dot(shifted[side, first : first + block, :], w_mid[tap, :, lanes])
                    total = term if total is None else total + term
                pre_two[at : at + block, lanes] = total
    saves.append(local(pre_two, pre_two_out, 14))

    local_part(pre_two, "conv", pay_two)
    spread = spread_of(pay_two, slots_two, 1)
    load_out.wait()
    for piece in range(4):
        low = piece * width // 16 * 16
        length = min(table.shape[0], channels - low)
        table[:length, :real] = kernel_out[low : low + length, :].astype(F32)
        off = piece * width - low
        block = table[off : off + group, :]
        block = jnp.where(row_of(block.shape) < width, block, 0.0)
        place = piece % 2 * group
        k_out[piece // 2, place : place + group, :] = block.astype(BF16)
    send_out = partner(k_out, k_out_both.at[core], base + 2)
    load_squeeze.wait()
    for piece in range(2):
        low = piece * width // 16 * 16
        length = min(table.shape[0], 2 * width - low)
        table[:length, :width] = squeeze[low : low + length, :].astype(F32)
        off = piece * width - low
        block = table[off : off + group, :group]
        keep = (row_of(block.shape) < width) & (lane_of(block.shape) < width)
        w_squeeze[piece * group : (piece + 1) * group, :] = jnp.where(keep, block, 0.0).astype(BF16)
    load_excite.wait()
    table[:width, :real] = excite[...].astype(F32)
    block = group_lanes(table[:group, :], plan)
    w_excite[...] = jnp.where(row_of(block.shape) < width, block, 0.0).astype(BF16)
    spread.wait()
    mean_two, variance, _ = merge_moments(slots_two, n, half)
    inverse_two = lax.rsqrt(variance + EPSILON)
    stats[MEAN_TWO : MEAN_TWO + 1, :] = mean_two
    stats[INVERSE_TWO : INVERSE_TWO + 1, :] = inverse_two
    scale_two = inverse_two * vec[GAIN_TWO : GAIN_TWO + 1, :]
    shift_two = vec[SHIFT_TWO : SHIFT_TWO + 1, :]
    pooled_out[...] = jnp.zeros_like(pooled_out)
    saves[1].wait()
    act_two = pre_one

    def activate_two(start, place, crop, carry):
        norm = (pre_two[pl.ds(place, TILE), :] - mean_two) * scale_two + shift_two
        act = norm * sigmoid(norm) * widen(mask[pl.ds(start, TILE), :], half)
        act_two[pl.ds(start, TILE), :] = act
        pooled_out[pl.ds(crop, 1), :] += jnp.sum(act, 0, keepdims=True)
        return carry

    plan.sweep(activate_two, 0)
    pooled_out[:1, :] = pooled_out[:1, :] * (1.0 / plan.glob_area)
    pooled_out[1:, :] = pooled_out[1:, :] * (1.0 / plan.slot_area)
    part = split_dot(pooled_out[...], w_squeeze[...])
    squeeze_send[...] = part
    swap = partner(squeeze_send, squeeze_recv, base + 3)
    swap.wait()
    squeeze_pre = part + squeeze_recv[...] + vec[SQUEEZE_BIAS : SQUEEZE_BIAS + 1, :group]
    squeeze_pre_out[...] = squeeze_pre
    squeezed = squeeze_pre * sigmoid(squeeze_pre)
    excite_out[...] = sigmoid(
        split_dot(squeezed, w_excite[...]) + vec[EXCITE_BIAS : EXCITE_BIAS + 1, :]
    )
    saves.append(local(w_in, w_in_both.at[core], 15))
    saves.append(local(k_out, k_out_both.at[core], 16))

    def activate_three(start, place, crop, carry):
        act_three[core, pl.ds(start, TILE), :] = (
            act_two[pl.ds(start, TILE), :] * excite_out[pl.ds(crop, 1), :]
        ).astype(BF16)
        return carry

    plan.sweep(activate_three, 0)
    exchange = partner(act_three.at[core], act_three.at[core], base + 4)
    saves.append(local(act_three.at[core], act_three_out.at[core], 17))
    for copy in (send_in, send_vec, send_out, exchange):
        copy.wait()
    saves.append(local(act_three.at[1 - core], act_three_out.at[1 - core], 18))
    for index, copy in enumerate(saves):
        if index != 1:
            copy.wait()


def forward(
    plan, live, glob, small, kernel_in, kernel_mid, kernel_out, squeeze, excite, vec_raw
):
    n, half, group = plan.dp, plan.half, plan.group
    shape = jax.ShapeDtypeStruct
    copies = 1 + plan.slots
    pay = 2 * half + LANE
    smem = pl.BlockSpec(memory_space=pltpu.SMEM)
    return pl.pallas_call(
        functools.partial(forward_kernel, plan),
        out_shape=(
            shape((2, plan.all, half), BF16),
            shape((plan.all, half), F32),
            shape((plan.conv, half), BF16),
            shape((plan.conv, half), F32),
            shape((2, plan.all, half), BF16),
            shape((3, 3 * group, half), BF16),
            shape((2, 2, half, half), BF16),
            shape((2, 2, half, half), BF16),
            shape((8, half), F32),
            shape((8, half), F32),
            shape((plan.all, LANE), F32),
            shape((half, group), BF16),
            shape((group, half), BF16),
            shape((8, half), F32),
            shape((plan.slot_rows, half), F32),
            shape((plan.slot_rows, half), F32),
            shape((plan.slot_rows, group), F32),
        ),
        in_specs=[smem] + [ANY] * 7 + [VMEM],
        out_specs=(ANY,) * 8 + (VMEM,) * 9,
        scratch_shapes=[
            pltpu.VMEM(glob.shape, BF16),
            pltpu.VMEM(small.shape, BF16),
            pltpu.VMEM(kernel_in.shape, BF16),
            pltpu.VMEM((3,) + kernel_mid.shape[1:], BF16),
            pltpu.VMEM(kernel_out.shape, BF16),
            pltpu.VMEM(squeeze.shape, BF16),
            pltpu.VMEM(excite.shape, BF16),
            pltpu.VMEM((32, 2 * half), F32),
            pltpu.VMEM((group + 16, half), F32),
            pltpu.VMEM((2, plan.all, half), BF16),
            pltpu.VMEM((plan.all, half), F32),
            pltpu.VMEM((2, plan.conv, 3 * group), BF16),
            pltpu.VMEM((2, half, half), BF16),
            pltpu.VMEM((3, 3 * group, half), BF16),
            pltpu.VMEM((plan.conv, half), F32),
            pltpu.VMEM((2, plan.all, half), BF16),
            pltpu.VMEM((2, half, half), BF16),
            pltpu.VMEM((1, pay), F32),
            pltpu.VMEM((n, 1, pay), F32),
            pltpu.VMEM((1, pay), F32),
            pltpu.VMEM((n, 1, pay), F32),
            pltpu.VMEM((plan.slot_rows, group), F32),
            pltpu.VMEM((plan.slot_rows, group), F32),
            pltpu.SemaphoreType.DMA((19,)),
            pltpu.SemaphoreType.DMA((copies + 5,)),
            pltpu.SemaphoreType.DMA((copies + 5,)),
            pltpu.SemaphoreType.DMA((2, n)),
            pltpu.SemaphoreType.DMA((2, n)),
        ],
        compiler_params=pltpu.CompilerParams(
            collective_id=0, has_side_effects=True, vmem_limit_bytes=VMEM_BYTES
        ),
    )(live, glob, small, kernel_in, kernel_mid, kernel_out, squeeze, excite, vec_raw)


def vector_table(vectors, plan):
    pieces = []
    for vector in vectors:
        size = 0
        if vector is not None:
            size = vector.shape[0]
            pieces.append(vector.astype(F32))
        if plan.half > size:
            pieces.append(jnp.zeros((plan.half - size,), F32))
    return jnp.concatenate(pieces).reshape(len(vectors), plan.half)


def own_steps(plan, body, carry):
    step = 32

    def run(tile, state):
        return body(pl.multiple_of(tile * step, step), step, state)

    return lax.fori_loop(0, plan.own // step, run, carry)


def merge_two(first, second, lanes):
    sums = [part[:, :lanes] for part in (first, second)]
    squares = [part[:, lanes : 2 * lanes] for part in (first, second)]
    counts = [widen(part[:, 2 * lanes :], lanes) for part in (first, second)]
    total = sums[0] + sums[1]
    count = counts[0] + counts[1]
    mean = total / count
    spread = squares[0] + squares[1]
    for index in range(2):
        gap = sums[index] / counts[index] - mean
        spread = spread + counts[index] * gap * gap
    return total, spread, count


def split_maps(plan, glob, small, target, wide):
    half, real = plan.half, plan.half_real
    low = real // LANE * LANE

    def place(source, row, start, size, real_size):
        wide[:real_size, : plan.channels] = source[row].astype(F32)
        rows = pl.ds(pl.multiple_of(start, 16), size)
        first = wide[:size, :half]
        target[0, rows, :] = jnp.where(lane_of(first.shape) < real, first, 0.0).astype(BF16)
        second = wide[:size, low:]
        moved = pltpu.roll(second, second.shape[1] - (real - low), 1)
        target[1, rows, :] = moved[:, :half].astype(BF16)

    def glob_row(row, carry):
        place(glob, row, row * plan.glob_width, plan.glob_width, plan.glob_side)
        return carry

    def small_row(row, carry):
        start = plan.glob_own + row * plan.small_width
        place(small, row, start, plan.small_width, plan.small_side)
        return carry

    wide[...] = jnp.zeros_like(wide)
    lax.fori_loop(0, plan.glob_height, glob_row, 0)
    wide[...] = jnp.zeros_like(wide)
    lax.fori_loop(0, plan.slots * plan.small_height, small_row, 0)


def third_kernel(
    plan,
    live,
    act_three_hbm,
    k_out_hbm,
    glob_hbm,
    small_hbm,
    glob_cot_hbm,
    small_cot_hbm,
    vec,
    vec_raw,
    vec_three_other,
    result_out,
    grad_summed_out,
    grad_pre_three_out,
    sums_out,
    act_three,
    k_out,
    pre_three,
    grad_summed,
    grad_pre_three,
    pay,
    pair,
    chip,
    slots,
    finals,
    pay_back,
    pair_back,
    chip_back,
    slots_back,
    finals_back,
    vec_three,
    glob,
    small,
    glob_cot,
    small_cot,
    x_own,
    cot_own,
    mask,
    wide,
    local_sem,
    send_sem,
    recv_sem,
    spread_send,
    spread_recv,
):
    n, half = plan.dp, plan.half
    me, core = lax.axis_index("dp"), lax.axis_index("rows")
    pieces = plan.own_pieces(core)

    def local(source, target, index):
        copy = pltpu.make_async_copy(source, target, local_sem.at[index])
        copy.start()
        return copy

    def partner(source, target, index):
        copy = to_partner(me, core, source, target, send_sem.at[index], recv_sem.at[index])
        copy.start()
        return copy

    loads = [
        local(
            act_three_hbm.at[:, pl.ds(place, length), :],
            act_three.at[:, pl.ds(start, length), :],
            index,
        )
        for index, (place, start, length) in enumerate(pieces)
    ]
    base = len(pieces)
    loads.append(local(k_out_hbm, k_out, base))
    raws = [
        local(source, target, 3 * base + 1 + index)
        for index, (source, target) in enumerate(
            (
                (glob_hbm, glob),
                (small_hbm, small),
                (glob_cot_hbm, glob_cot),
                (small_cot_hbm, small_cot),
            )
        )
    ]
    entry_barrier(n, me, core)
    vec_three[core] = vec_raw[8:, :]
    vec_three[1 - core] = vec_three_other[...]
    fill_mask(plan, mask, plan.glob_own, plan.slot_own, live[0].astype(F32))
    for copy in loads:
        copy.wait()
    own_count = 0.5 * vec[COUNT : COUNT + 1, :]

    block = plan.own // 2
    for side in range(2):

        def product(part, carry, side=side):
            rows = pl.ds(pl.multiple_of(part * block, 16), block)
            pre_three[side, rows, :] = dot(act_three[0, rows, :], k_out[side, 0]) + dot(
                act_three[1, rows, :], k_out[side, 1]
            )
            return carry

        lax.fori_loop(0, 2, product, 0)

    for side in range(2):

        def add(row, step, carry, side=side):
            rows = pl.ds(row, step)
            return carry + rows_down(pre_three[side, rows, :] * widen(mask[rows, :], half))

        total = jnp.sum(own_steps(plan, add, jnp.zeros((8, half), F32)), 0, keepdims=True)
        mean = total / own_count

        def spread(row, step, carry, side=side, mean=mean):
            rows = pl.ds(row, step)
            gap = (pre_three[side, rows, :] - mean) * widen(mask[rows, :], half)
            return carry + rows_down(gap * gap)

        squares = jnp.sum(own_steps(plan, spread, jnp.zeros((8, half), F32)), 0, keepdims=True)
        pay[side, :, :half] = total
        pay[side, :, half : 2 * half] = squares
        pay[side, :, 2 * half :] = own_count[:, :LANE]
    partner(pay.at[1 - core], pair, 0).wait()
    total, squares, count = merge_two(pay[core], pair[...], half)
    chip[:, :half] = total
    chip[:, half : 2 * half] = squares
    chip[:, 2 * half :] = count[:, :LANE]
    exchange = Spread(n, me, core, chip, slots, spread_send.at[0], spread_recv.at[0])
    exchange.start()
    for copy in raws:
        copy.wait()
    split_maps(plan, glob, small, x_own, wide)
    split_maps(plan, glob_cot, small_cot, cot_own, wide)
    exchange.wait()
    mean, variance, full_count = merge_moments(slots, n, half)
    finals[core, :, :half] = mean
    finals[core, :, half:] = lax.rsqrt(variance + EPSILON)
    partner(finals.at[core], finals.at[core], 1).wait()

    for side in range(2):
        mean = finals[side, :, :half]
        inverse = finals[side, :, half:]
        gain = vec_three[side, :1, :]
        shift = vec_three[side, 1:2, :]

        def outer(row, step, carry, side=side, mean=mean, inverse=inverse, gain=gain, shift=shift):
            rows = pl.ds(row, step)
            seen = widen(mask[rows, :], half)
            normed = (pre_three[side, rows, :] - mean) * inverse
            summed = normed * gain + shift + x_own[side, rows, :].astype(F32)
            sigma = sigmoid(summed)
            result_out[side, rows, :] = (seen * summed * sigma).astype(BF16)
            slope = sigma * (1.0 + summed * (1.0 - sigma))
            grad = cot_own[side, rows, :].astype(F32) * seen * slope
            grad_summed[side, rows, :] = grad
            grad_summed_out[side, rows, :] = grad.astype(BF16)
            return carry[0] + rows_down(grad), carry[1] + rows_down(grad * normed)

        zero = jnp.zeros((8, half), F32)
        shift_sum, gain_sum = own_steps(plan, outer, (zero, zero))
        pay_back[side, :, :half] = jnp.sum(shift_sum, 0, keepdims=True)
        pay_back[side, :, half:] = jnp.sum(gain_sum, 0, keepdims=True)
    partner(pay_back.at[1 - core], pair_back, 2).wait()
    chip_back[...] = pay_back[core] + pair_back[...]
    exchange = Spread(n, me, core, chip_back, slots_back, spread_send.at[1], spread_recv.at[1])
    exchange.start()
    exchange.wait()

    finals_back[core] = gather_sum(slots_back, n, 2 * half)
    partner(finals_back.at[core], finals_back.at[core], 3).wait()
    copies = []
    for side in range(2):
        mean = finals[side, :, :half]
        inverse = finals[side, :, half:]
        shift_sum = finals_back[side, :, :half]
        gain_sum = finals_back[side, :, half:]
        sums_out[side] = jnp.concatenate([shift_sum, gain_sum, jnp.zeros((6, half), F32)], 0)
        scale = vec_three[side, :1, :] * inverse
        shift_mean = shift_sum / full_count
        gain_mean = gain_sum / full_count

        def inner(
            row, step, carry, side=side, mean=mean, inverse=inverse, scale=scale,
            shift_mean=shift_mean, gain_mean=gain_mean
        ):
            rows = pl.ds(row, step)
            normed = (pre_three[side, rows, :] - mean) * inverse
            grad = scale * (grad_summed[side, rows, :] - shift_mean - normed * gain_mean)
            grad_pre_three[side, rows, :] = (grad * widen(mask[rows, :], half)).astype(BF16)
            return carry

        own_steps(plan, inner, 0)
        for index, (place, start, length) in enumerate(pieces):
            source = grad_pre_three.at[side, pl.ds(start, length), :]
            target = grad_pre_three_out.at[side, pl.ds(place, length), :]
            copies.append(partner(source, target, 4 + side * base + index))
            copies.append(local(source, target, base + 1 + side * base + index))
    for copy in copies:
        copy.wait()


def gather_sum(slots, n, lanes):
    def add(step, carry):
        return carry + slots[step]

    return lax.fori_loop(0, n, add, jnp.zeros((1, lanes), F32))


def third(
    plan, live, act_three, k_out, glob, small, glob_cot, small_cot, vec, vec_raw, vec_three_other
):
    n, half = plan.dp, plan.half
    shape = jax.ShapeDtypeStruct
    pieces = 1 + plan.slots
    pay = 2 * half + LANE
    own = (2, plan.own, half)
    return pl.pallas_call(
        functools.partial(third_kernel, plan),
        out_shape=(
            shape(own, BF16),
            shape(own, BF16),
            shape((2, plan.all, half), BF16),
            shape((2, 8, half), F32),
        ),
        in_specs=[pl.BlockSpec(memory_space=pltpu.SMEM)] + [ANY] * 6 + [VMEM] * 3,
        out_specs=(VMEM, VMEM, ANY, VMEM),
        scratch_shapes=[
            pltpu.VMEM(own, BF16),
            pltpu.VMEM(k_out.shape, BF16),
            pltpu.VMEM(own, F32),
            pltpu.VMEM(own, F32),
            pltpu.VMEM(own, BF16),
            pltpu.VMEM((2, 1, pay), F32),
            pltpu.VMEM((1, pay), F32),
            pltpu.VMEM((1, pay), F32),
            pltpu.VMEM((n, 1, pay), F32),
            pltpu.VMEM((2, 1, 2 * half), F32),
            pltpu.VMEM((2, 1, 2 * half), F32),
            pltpu.VMEM((1, 2 * half), F32),
            pltpu.VMEM((1, 2 * half), F32),
            pltpu.VMEM((n, 1, 2 * half), F32),
            pltpu.VMEM((2, 1, 2 * half), F32),
            pltpu.VMEM((2,) + vec_three_other.shape, F32),
            pltpu.VMEM(glob.shape, BF16),
            pltpu.VMEM(small.shape, BF16),
            pltpu.VMEM(glob.shape, BF16),
            pltpu.VMEM(small.shape, BF16),
            pltpu.VMEM(own, BF16),
            pltpu.VMEM(own, BF16),
            pltpu.VMEM((plan.own, LANE), F32),
            pltpu.VMEM((32, 2 * half), F32),
            pltpu.SemaphoreType.DMA((3 * pieces + 5,)),
            pltpu.SemaphoreType.DMA((2 * pieces + 4,)),
            pltpu.SemaphoreType.DMA((2 * pieces + 4,)),
            pltpu.SemaphoreType.DMA((2, n)),
            pltpu.SemaphoreType.DMA((2, n)),
        ],
        compiler_params=pltpu.CompilerParams(
            collective_id=1, has_side_effects=True, vmem_limit_bytes=VMEM_BYTES
        ),
    )(live, act_three, k_out, glob, small, glob_cot, small_cot, vec, vec_raw, vec_three_other)


ORDERS = {
    "A": ((0, 1, 2, 3), (1, 0, 2, 3)),
    "B": ((0, 2, 1, 3), (1, 2, 0, 3)),
    "P": ((0, 1, 2, 3), (2, 1, 0, 3)),
    "Q": ((2, 0, 1, 3), (1, 0, 2, 3)),
}
HANDED = 2


class Steps:
    def __init__(self, n, me, core, order):
        bits = n.bit_length() - 1
        self.halvings = min(bits, 4)
        self.shards = 2**self.halvings
        self.doublings = bits - self.halvings
        self.bit, self.partner = [], []
        chosen = [[bit for bit in one if bit < bits] for one in ORDERS[order]]
        chosen = [one + list(range(self.halvings, bits)) for one in chosen]
        for step in range(bits):
            first, second = 2 ** chosen[0][step], 2 ** chosen[1][step]
            distance = first + (second - first) * core
            bit = lax.rem(me // distance, 2)
            self.bit.append(bit)
            self.partner.append((me + distance * (1 - 2 * bit), core))


class Chain:
    def __init__(self, steps, work, land, send, recv, free, begun=0, until=None):
        self.steps, self.work, self.land, self.free = steps, work, land, free
        self.send, self.recv = send, recv
        self.rows = work.shape[0]
        self.shard = self.rows // steps.shards
        self.halvings = steps.halvings
        self.reduce_steps = steps.halvings + steps.doublings
        self.begun, self.until = begun, until
        self.pending = None
        self.step, self.at, self.length = begun, 0, self.rows >> begun
        for step in range(begun):
            self.at = self.at + steps.bit[step] * (self.rows >> (step + 1))
        self.land_base = self.rows - self.length
        self.back = None

    def rows_at(self, row, length):
        return pl.ds(row if isinstance(row, int) else pl.multiple_of(row, 16), length)

    def here(self):
        return self.work.at[self.rows_at(self.at, self.length), :]

    def remote(self, source, target, step, slot):
        self.pending = pltpu.make_async_remote_copy(
            src_ref=source,
            dst_ref=target,
            send_sem=self.send.at[slot],
            recv_sem=self.recv.at[slot],
            device_id=self.steps.partner[step],
            device_id_type=MESH,
        )
        self.pending.start()

    def begin_reduce(self):
        step = self.step
        if step < self.halvings:
            length = self.rows >> (step + 1)
            bit = self.steps.bit[step]
            self.keep = self.at + bit * length
            gone = self.at + (1 - bit) * length
            low = self.rows - 2 * length
        else:
            length = self.shard
            self.keep = gone = self.at
            low = self.rows - self.shard + (step - self.halvings) * self.shard
        self.length = length
        self.landed = self.land.at[pl.ds(low - self.land_base, length), :]
        self.remote(self.work.at[self.rows_at(gone, length), :], self.landed, step, step)

    def end_reduce(self):
        self.pending.wait()
        if self.free is not None and self.step < self.halvings:
            pl.semaphore_signal(
                self.free.at[self.step],
                inc=1,
                device_id=self.steps.partner[self.step],
                device_id_type=MESH,
            )
        size = 48 if self.shard % 48 == 0 else 16

        def add(tile, carry):
            there = self.rows_at(self.keep + tile * size, size)
            here = pl.ds(pl.multiple_of(tile * size, 16), size)
            total = self.work[there, :].astype(F32) + self.landed[here, :].astype(F32)
            self.work[there, :] = total.astype(BF16)
            return carry

        lax.fori_loop(0, self.length // size, add, 0)
        self.at = self.keep
        self.step += 1

    def begin_gather(self):
        if self.back >= self.begun:
            pl.semaphore_wait(self.free.at[self.back], 1)
        part = self.here()
        self.remote(part, part, self.back, self.reduce_steps + self.back)

    def end_gather(self):
        self.pending.wait()
        self.at = self.at - self.steps.bit[self.back] * self.length
        self.length *= 2
        self.back -= 1

    def advance(self):
        if self.pending is not None:
            if self.back is None:
                self.end_reduce()
            else:
                self.end_gather()
            self.pending = None
        if self.step == self.until:
            return
        if self.step < self.reduce_steps:
            self.begin_reduce()
            return
        if self.back is None:
            self.back = self.halvings - 1
        if self.back >= 0:
            self.begin_gather()

    def done(self):
        return self.pending is None and (self.step == self.until or self.back == -1)


def land_rows(n, rows, begun=0, until=None):
    bits = n.bit_length() - 1
    halvings = min(bits, 4)
    last = halvings if until is None else min(until, halvings)
    extra = bits - halvings if until is None else 0
    return (rows >> begun) - (rows >> last) + extra * (rows >> halvings)


def chain_slots(n):
    bits = n.bit_length() - 1
    return bits + min(bits, 4)


def silu_slope(value, sigma):
    return sigma * (1.0 + value * (1.0 - sigma))
SHIFT_TWO_SUM, GAIN_TWO_SUM, EXCITE_SUM, SQUEEZE_SUM = range(4)
SHIFT_ONE_SUM, GAIN_ONE_SUM = range(2)


def second_kernel(
    plan,
    grad_pre_three_hbm,
    act_three_hbm,
    k_out_hbm,
    pre_two_hbm,
    stats,
    vec,
    mask,
    pooled,
    excite,
    squeeze_pre,
    w_squeeze,
    w_excite,
    shard_out,
    grad_norm_out,
    grad_excite_out,
    grad_squeeze_out,
    sums_out,
    grad_pre_three,
    act_three,
    k_out,
    pre_two,
    grad_act,
    slopes,
    work,
    land,
    grad_excite,
    squeeze_send,
    squeeze_recv,
    grad_pooled,
    factors,
    factor_slots,
    pay,
    slots,
    local_sem,
    pair_send,
    pair_recv,
    spread_send,
    spread_recv,
    reduce_send,
    reduce_recv,
):
    n, half, group = plan.dp, plan.half, plan.group
    me, core = lax.axis_index("dp"), lax.axis_index("rows")
    entry_barrier(n, me, core)

    def local(source, target, index):
        copy = pltpu.make_async_copy(source, target, local_sem.at[index])
        copy.start()
        return copy

    loads = [
        local(grad_pre_three_hbm, grad_pre_three, 0),
        local(act_three_hbm, act_three, 1),
        local(k_out_hbm.at[:, core], k_out, 2),
        local(pre_two_hbm, pre_two, 3),
    ]
    loads[0].wait()
    loads[1].wait()
    for side in range(2):
        for part in range(2):
            lanes = slice(part * group, (part + 1) * group)
            low = side * half + part * group
            work[low : low + group, :] = dot_tn(
                act_three[side, :, lanes], grad_pre_three[core]
            ).astype(BF16)
    reduction = Chain(
        Steps(n, me, core, ORDER_OUT), work, land, reduce_send, reduce_recv, None, until=HANDED
    )
    reduction.advance()
    loads[2].wait()

    block = plan.all // 4

    def product(part, carry):
        rows = pl.ds(pl.multiple_of(part * block, 16), block)
        grad_act[rows, :] = dot_nt(grad_pre_three[0, rows, :], k_out[0]) + dot_nt(
            grad_pre_three[1, rows, :], k_out[1]
        )
        return carry

    lax.fori_loop(0, 4, product, 0)
    loads[3].wait()

    mean = stats[MEAN_TWO : MEAN_TWO + 1, :]
    inverse = stats[INVERSE_TWO : INVERSE_TWO + 1, :]
    count = stats[TOTAL : TOTAL + 1, :]
    gain = vec[GAIN_TWO : GAIN_TWO + 1, :]
    shift = vec[SHIFT_TWO : SHIFT_TWO + 1, :]
    grad_excite[...] = jnp.zeros_like(grad_excite)

    def excitation(start, place, crop, carry):
        rows = pl.ds(start, TILE)
        norm = (pre_two[pl.ds(place, TILE), :] - mean) * (inverse * gain) + shift
        sigma = sigmoid(norm)
        seen = widen(mask[rows, :], half)
        slopes[rows, :] = silu_slope(norm, sigma) * seen
        term = grad_act[rows, :] * (norm * sigma * seen)
        grad_excite[pl.ds(crop, 1), :] += jnp.sum(term, 0, keepdims=True)
        return carry

    plan.sweep(excitation, 0)
    level = excite[...]
    grad_excite_pre = grad_excite[...] * level * (1.0 - level)
    part = split_dot(grad_excite_pre, w_excite[...], nt=True)
    squeeze_send[...] = part
    swap = to_partner(me, core, squeeze_send, squeeze_recv, pair_send.at[0], pair_recv.at[0])
    swap.start()
    reduction.advance()
    swap.wait()
    before = squeeze_pre[...]
    sigma = sigmoid(before)
    squeezed = before * sigma
    grad_squeeze_pre = (part + squeeze_recv[...]) * silu_slope(before, sigma)
    back = split_dot(grad_squeeze_pre, w_squeeze[...], nt=True)
    crop_row = lax.broadcasted_iota(jnp.int32, back.shape, 0)
    area = jnp.where(crop_row == 0, 1.0 / plan.glob_area, 1.0 / plan.slot_area)
    grad_pooled[...] = back * area
    deep = plan.slot_rows
    factors[:deep, :group] = squeezed.astype(BF16)
    factors[:deep, group:] = grad_excite_pre.astype(BF16)
    factors[deep:, :group] = grad_squeeze_pre.astype(BF16)
    factors[deep:, group:] = pooled[...].astype(BF16)
    factor_spread = Spread(n, me, core, factors, factor_slots, spread_send.at[0], spread_recv.at[0])
    factor_spread.start()

    def gradient(start, place, crop, carry):
        rows = pl.ds(start, TILE)
        incoming = grad_act[rows, :] * excite[pl.ds(crop, 1), :] + grad_pooled[pl.ds(crop, 1), :]
        grad = incoming * slopes[rows, :]
        grad_act[rows, :] = grad
        normed = (pre_two[pl.ds(place, TILE), :] - mean) * inverse
        return carry[0] + rows_down(grad), carry[1] + rows_down(grad * normed)

    zero = jnp.zeros((8, half), F32)
    shift_sum, gain_sum = plan.sweep(gradient, (zero, zero))
    save = local(grad_act, grad_norm_out, 4)
    pay[:, :half] = jnp.sum(shift_sum, 0, keepdims=True)
    pay[:, half:] = jnp.sum(gain_sum, 0, keepdims=True)
    spread = Spread(n, me, core, pay, slots, spread_send.at[1], spread_recv.at[1])
    spread.start()
    while not reduction.done():
        reduction.advance()
    store = local(reduction.here(), shard_out, 5)
    factor_spread.wait()
    left = factor_slots[:, :, :group].reshape(n * 2 * deep, group)
    right = factor_slots[:, :, group:].reshape(n * 2 * deep, half)
    upper = lax.broadcasted_iota(jnp.int32, left.shape, 0) % (2 * deep) < deep
    zeros = jnp.zeros_like(left)
    excite_left = jnp.where(upper, left, zeros)
    squeeze_left = jnp.where(upper, zeros, left)
    grad_excite_out[...] = dot_tn(excite_left, right)
    grad_squeeze_out[...] = dot_tn(right, squeeze_left)
    wide_upper = lax.broadcasted_iota(jnp.int32, right.shape, 0) % (2 * deep) < deep
    excite_bias = jnp.sum(jnp.where(wide_upper, right.astype(F32), 0.0), 0, keepdims=True)
    squeeze_bias = jnp.sum(squeeze_left.astype(F32), 0, keepdims=True)
    spread.wait()
    totals = gather_sum(slots, n, 2 * half)
    sums_out[...] = jnp.zeros_like(sums_out)
    sums_out[SHIFT_TWO_SUM : SHIFT_TWO_SUM + 1, :] = totals[:, :half]
    sums_out[GAIN_TWO_SUM : GAIN_TWO_SUM + 1, :] = totals[:, half:]
    sums_out[EXCITE_SUM : EXCITE_SUM + 1, :] = excite_bias
    sums_out[SQUEEZE_SUM : SQUEEZE_SUM + 1, :group] = squeeze_bias
    save.wait()
    store.wait()


def second(
    plan, grad_pre_three, act_three, k_out, pre_two, stats, vec, mask, pooled, excite,
    squeeze_pre, w_squeeze, w_excite
):
    n, half, group = plan.dp, plan.half, plan.group
    shape = jax.ShapeDtypeStruct
    rows = 2 * half
    shard = rows >> HANDED
    deep = plan.slot_rows
    bits = n.bit_length() - 1
    return pl.pallas_call(
        functools.partial(second_kernel, plan),
        out_shape=(
            shape((shard, half), BF16),
            shape((plan.all, half), F32),
            shape((group, half), F32),
            shape((half, group), F32),
            shape((8, half), F32),
        ),
        in_specs=[ANY] * 4 + [VMEM] * 8,
        out_specs=(ANY, ANY, VMEM, VMEM, VMEM),
        scratch_shapes=[
            pltpu.VMEM((2, plan.all, half), BF16),
            pltpu.VMEM((2, plan.all, half), BF16),
            pltpu.VMEM((2, half, half), BF16),
            pltpu.VMEM((plan.conv, half), F32),
            pltpu.VMEM((plan.all, half), F32),
            pltpu.VMEM((plan.all, half), F32),
            pltpu.VMEM((rows, half), BF16),
            pltpu.VMEM((land_rows(n, rows, until=HANDED), half), BF16),
            pltpu.VMEM((deep, half), F32),
            pltpu.VMEM((deep, group), F32),
            pltpu.VMEM((deep, group), F32),
            pltpu.VMEM((deep, half), F32),
            pltpu.VMEM((2 * deep, group + half), BF16),
            pltpu.VMEM((n, 2 * deep, group + half), BF16),
            pltpu.VMEM((1, 2 * half), F32),
            pltpu.VMEM((n, 1, 2 * half), F32),
            pltpu.SemaphoreType.DMA((6,)),
            pltpu.SemaphoreType.DMA((1,)),
            pltpu.SemaphoreType.DMA((1,)),
            pltpu.SemaphoreType.DMA((2, n)),
            pltpu.SemaphoreType.DMA((2, n)),
            pltpu.SemaphoreType.DMA((bits,)),
            pltpu.SemaphoreType.DMA((bits,)),
        ],
        compiler_params=pltpu.CompilerParams(
            collective_id=2, has_side_effects=True, vmem_limit_bytes=VMEM_BYTES
        ),
    )(
        grad_pre_three, act_three, k_out, pre_two, stats, vec, mask, pooled, excite, squeeze_pre,
        w_squeeze, w_excite
    )


CHAINS = ("out", "mid0", "mid1", "mid2", "in0", "in1")
ORDER_OUT = "A"
CHAIN_ORDERS = (ORDER_OUT, "B", "P", "Q", "P", "Q")
SCHEDULE = (
    "two", "M0", "M1", "C0", "out", "C1", "C2", "C3", "C4", "C5", "mid0", "out", "mid1", "C6",
    "C7", "sums", "out", "M2", "mid1", "out", "one", "K0", "mid2", "mid0", "mid1", "K1",
    "mid1", "mid2", "in0", "mid0", "mid1", "mid0", "X0", "X1", "in1", "in0", "mid2", "mid0",
    "out", "mid1", "mid2", "in1", "mid2", "X2", "mid0", "in0", "in0", "mid2", "mid1", "in1",
    "in0", "in1", "mid2", "in1", "in1", "in0", "mid0", "mid1", "X3", "in1", "in0", "mid2",
    "out", "mid0", "in0", "in1",
)


def first_kernel(
    plan,
    shard_out_hbm,
    grad_norm_hbm,
    pre_two_hbm,
    pre_one_hbm,
    act_one_hbm,
    x_hbm,
    w_mid_hbm,
    w_in_hbm,
    stats,
    vec,
    sums_two,
    mask,
    gathered_out,
    gathered_mid,
    gathered_in,
    grad_inputs_out,
    sums_out,
    flat,
    conv_rows,
    shifted,
    act_one,
    w_mid,
    grad_pre_one,
    grad_other,
    w_in,
    work_out,
    land_out,
    work_mid,
    land_mid,
    work_in,
    land_in,
    pay,
    slots,
    local_sem,
    pair_send,
    pair_recv,
    spread_send,
    spread_recv,
    chain_send,
    chain_recv,
    free,
):
    n, half, group = plan.dp, plan.half, plan.group
    me, core = lax.axis_index("dp"), lax.axis_index("rows")
    entry_barrier(n, me, core)

    def local(source, target, index):
        copy = pltpu.make_async_copy(source, target, local_sem.at[index])
        copy.start()
        return copy

    chains, targets, saves, waits, state = {}, {}, {}, {}, {}

    def begin(name, work, land, target, begun=0):
        index = CHAINS.index(name)
        steps = Steps(n, me, core, CHAIN_ORDERS[index])
        chains[name] = Chain(
            steps, work, land, chain_send.at[index], chain_recv.at[index], free.at[index], begun
        )
        targets[name] = target
        return chains[name]

    def advance(name):
        chain = chains[name]
        if name in saves:
            return
        chain.advance()
        if chain.done():
            index = CHAINS.index(name)
            saves[name] = local(chain.work, targets[name], 8 + index)

    out = begin("out", work_out, land_out, gathered_out, HANDED)
    load_shard = local(shard_out_hbm, out.here(), 2)
    waits["norm"] = local(grad_norm_hbm, flat, 0)
    waits["two"] = local(pre_two_hbm, conv_rows, 1)
    waits["act"] = local(act_one_hbm, act_one, 3)
    waits["mid"] = local(w_mid_hbm, w_mid, 4)
    waits["in"] = local(w_in_hbm, w_in, 5)
    load_shard.wait()
    advance("out")
    count = stats[TOTAL : TOTAL + 1, :]

    def norm_two():
        zero_borders(plan, shifted)
        mean = stats[MEAN_TWO : MEAN_TWO + 1, :]
        inverse = stats[INVERSE_TWO : INVERSE_TWO + 1, :]
        scale = vec[GAIN_TWO : GAIN_TWO + 1, :] * inverse
        shift_mean = sums_two[SHIFT_TWO_SUM : SHIFT_TWO_SUM + 1, :] / count
        gain_mean = sums_two[GAIN_TWO_SUM : GAIN_TWO_SUM + 1, :] / count * inverse
        waits["norm"].wait()
        waits["two"].wait()

        def into_two(start, place, crop, carry):
            rows = pl.ds(start, TILE)
            centered = conv_rows[pl.ds(place, TILE), :] - mean
            grad = scale * (flat[rows, :] - shift_mean - centered * gain_mean)
            grad = grad * widen(mask[rows, :], half)
            after = pltpu.roll(grad, TILE - 1, 0)
            before = pltpu.roll(grad, 1, 0)
            for tap, value in enumerate((after, grad, before)):
                for side in range(2):
                    shifted[side, pl.ds(place, TILE), tap * group : (tap + 1) * group] = value[
                        :, side * group : (side + 1) * group
                    ].astype(BF16)
            return carry

        plan.sweep(into_two, 0)
        waits["one"] = local(pre_one_hbm, flat, 0)
        waits["act"].wait()

    def mid(tap):
        for side in range(2):
            lanes = slice(side * group, (side + 1) * group)
            total = None
            for low, length, width in plan.segments():
                first = low - (tap - 1) * width
                term = dot_tn(
                    act_one[low : low + length, lanes], shifted[side, first : first + length, :]
                )
                total = term if total is None else total + term
            work_mid[tap, lanes, :] = total.astype(BF16)
        name = CHAINS[1 + tap]
        begin(name, work_mid.at[tap], land_mid.at[tap], gathered_mid.at[tap])
        advance(name)
        read_shifted()

    def read_shifted():
        state["reads"] = state.get("reads", 0) + 1
        if state["reads"] == 3 + 8:
            waits["x"] = local(x_hbm, shifted.at[:, pl.ds(0, plan.all), pl.ds(0, half)], 7)

    def conv(index):
        if index == 0:
            waits["mid"].wait()
        low, length, width = plan.segments()[index // 4]
        block = length // 2
        side = index // 2 % 2
        at = low + index % 2 * block
        lanes = slice(side * group, (side + 1) * group)
        total = None
        for tap in range(3):
            first = at - (tap - 1) * width
            for column in range(3):
                taps = slice(column * group, (column + 1) * group)
                term = dot_nt(shifted[side, first : first + block, taps], w_mid[tap, taps, lanes])
                total = term if total is None else total + term
        conv_rows[at : at + block, lanes] = total
        read_shifted()

    mean = stats[MEAN_ONE : MEAN_ONE + 1, :]
    inverse = stats[INVERSE_ONE : INVERSE_ONE + 1, :]
    gain = vec[GAIN_ONE : GAIN_ONE + 1, :]
    shift = vec[SHIFT_ONE : SHIFT_ONE + 1, :]
    spread = Spread(n, me, core, pay, slots, spread_send, spread_recv)

    def sums_one():
        waits["one"].wait()

        def gradient(start, place, crop, carry):
            rows = pl.ds(start, TILE)
            normed = (flat[rows, :] - mean) * inverse
            norm = normed * gain + shift
            sigma = sigmoid(norm)
            grad = conv_rows[pl.ds(place, TILE), :] * silu_slope(norm, sigma)
            grad = grad * widen(mask[rows, :], half)
            conv_rows[pl.ds(place, TILE), :] = grad
            return carry[0] + rows_down(grad), carry[1] + rows_down(grad * normed)

        zero = jnp.zeros((8, half), F32)
        shift_sum, gain_sum = plan.sweep(gradient, (zero, zero))
        pay[:, :half] = jnp.sum(shift_sum, 0, keepdims=True)
        pay[:, half:] = jnp.sum(gain_sum, 0, keepdims=True)
        spread.start()

    def norm_one():
        spread.wait()
        totals = gather_sum(slots, n, 2 * half)
        sums_out[...] = jnp.zeros_like(sums_out)
        sums_out[SHIFT_ONE_SUM : SHIFT_ONE_SUM + 1, :] = totals[:, :half]
        sums_out[GAIN_ONE_SUM : GAIN_ONE_SUM + 1, :] = totals[:, half:]
        scale = gain * inverse
        shift_mean = totals[:, :half] / count
        gain_mean = totals[:, half:] / count * inverse

        def into_one(start, place, crop, carry):
            rows = pl.ds(start, TILE)
            centered = flat[rows, :] - mean
            grad = scale * (conv_rows[pl.ds(place, TILE), :] - shift_mean - centered * gain_mean)
            grad_pre_one[rows, :] = (grad * widen(mask[rows, :], half)).astype(BF16)
            return carry

        plan.sweep(into_one, 0)
        state["swaps"] = []
        for index, (place, start, length) in enumerate(plan.own_pieces(1 - core)):
            swap = to_partner(
                me,
                core,
                grad_pre_one.at[pl.ds(place, length), :],
                grad_other.at[pl.ds(start, length), :],
                pair_send.at[index],
                pair_recv.at[index],
            )
            swap.start()
            state["swaps"].append(swap)

    def kernel_in(side):
        if side == 0:
            waits["x"].wait()
        for part in range(2):
            lanes = slice(part * group, (part + 1) * group)
            work_in[side, lanes, :] = dot_tn(
                shifted[side, : plan.all, lanes], grad_pre_one[...]
            ).astype(BF16)
        name = CHAINS[4 + side]
        begin(name, work_in.at[side], land_in.at[side], gathered_in.at[side])
        advance(name)

    def inputs(index):
        if index == 0:
            waits["in"].wait()
            for swap in state["swaps"]:
                swap.wait()
        part, side = index // 2, index % 2
        marks = (0, plan.glob_own, plan.own)
        rows = slice(marks[part], marks[part + 1])
        pieces = plan.own_pieces(core)
        pieces = pieces[:1] if part == 0 else pieces[1:]
        own = jnp.concatenate([grad_pre_one[pl.ds(spot, size), :] for spot, _, size in pieces], 0)
        grad_inputs_out[side, rows, :] = (
            dot_nt(own, w_in[core, side]) + dot_nt(grad_other[rows, :], w_in[1 - core, side])
        ).astype(BF16)

    blocks = {
        "two": norm_two,
        "sums": sums_one,
        "one": norm_one,
    }
    for tap in range(3):
        blocks["M%d" % tap] = functools.partial(mid, tap)
    for index in range(8):
        blocks["C%d" % index] = functools.partial(conv, index)
    for side in range(2):
        blocks["K%d" % side] = functools.partial(kernel_in, side)
    for index in range(4):
        blocks["X%d" % index] = functools.partial(inputs, index)
    for item in SCHEDULE:
        if item in blocks:
            blocks[item]()
        else:
            advance(item)
    while len(saves) < len(CHAINS):
        for name in CHAINS:
            advance(name)
    for name in CHAINS:
        saves[name].wait()


def first(
    plan, shard_out, grad_norm, pre_two, pre_one, act_one, x_all, w_mid, w_in, stats, vec,
    sums_two, mask
):
    n, half, group = plan.dp, plan.half, plan.group
    shape = jax.ShapeDtypeStruct
    pieces = 1 + plan.slots
    return pl.pallas_call(
        functools.partial(first_kernel, plan),
        out_shape=(
            shape((2 * half, half), BF16),
            shape((3, half, 3 * group), BF16),
            shape((2, half, half), BF16),
            shape((2, plan.own, half), BF16),
            shape((8, half), F32),
        ),
        in_specs=[ANY] * 8 + [VMEM] * 4,
        out_specs=(ANY, ANY, ANY, VMEM, VMEM),
        scratch_shapes=[
            pltpu.VMEM((plan.all, half), F32),
            pltpu.VMEM((plan.conv, half), F32),
            pltpu.VMEM((2, plan.conv, 3 * group), BF16),
            pltpu.VMEM((plan.conv, half), BF16),
            pltpu.VMEM(w_mid.shape, BF16),
            pltpu.VMEM((plan.all, half), BF16),
            pltpu.VMEM((plan.own, half), BF16),
            pltpu.VMEM(w_in.shape, BF16),
            pltpu.VMEM((2 * half, half), BF16),
            pltpu.VMEM((land_rows(n, 2 * half, begun=HANDED), half), BF16),
            pltpu.VMEM((3, half, 3 * group), BF16),
            pltpu.VMEM((3, land_rows(n, half), 3 * group), BF16),
            pltpu.VMEM((2, half, half), BF16),
            pltpu.VMEM((2, land_rows(n, half), half), BF16),
            pltpu.VMEM((1, 2 * half), F32),
            pltpu.VMEM((n, 1, 2 * half), F32),
            pltpu.SemaphoreType.DMA((14,)),
            pltpu.SemaphoreType.DMA((pieces,)),
            pltpu.SemaphoreType.DMA((pieces,)),
            pltpu.SemaphoreType.DMA((n,)),
            pltpu.SemaphoreType.DMA((n,)),
            pltpu.SemaphoreType.DMA((len(CHAINS), chain_slots(n))),
            pltpu.SemaphoreType.DMA((len(CHAINS), chain_slots(n))),
            pltpu.SemaphoreType.REGULAR((len(CHAINS), 4)),
        ],
        compiler_params=pltpu.CompilerParams(
            collective_id=3, has_side_effects=True, vmem_limit_bytes=VMEM_BYTES
        ),
    )(
        shard_out, grad_norm, pre_two, pre_one, act_one, x_all, w_mid, w_in, stats, vec, sums_two,
        mask
    )


def join_lanes(low, high, real):
    zeros = jnp.zeros_like(low)
    wide = jnp.concatenate([low, zeros], 1)
    moved = pltpu.roll(jnp.concatenate([high, zeros], 1), real, 1)
    lane = lax.broadcasted_iota(jnp.int32, wide.shape, 1)
    return jnp.where(lane < real, wide, moved)


def finish_kernel(
    plan,
    result_hbm,
    grad_summed_hbm,
    grad_inputs_hbm,
    out_hbm,
    in_hbm,
    mid_hbm,
    excite,
    squeeze,
    glob_out_hbm,
    small_out_hbm,
    glob_grad_hbm,
    small_grad_hbm,
    kernel_in_hbm,
    kernel_mid_hbm,
    kernel_out_hbm,
    squeeze_out,
    excite_out,
    result,
    grad_summed,
    grad_inputs,
    packed_out,
    packed_in,
    packed_mid,
    glob_out,
    small_out,
    glob_grad,
    small_grad,
    kernel_in,
    kernel_mid,
    kernel_out,
    load_sem,
    store_sem,
):
    half, group, width, real = plan.half, plan.group, plan.width, plan.half_real
    loads, stores = {}, []
    sources = (
        (mid_hbm, packed_mid),
        (out_hbm, packed_out),
        (in_hbm, packed_in),
        (result_hbm, result),
        (grad_summed_hbm, grad_summed),
        (grad_inputs_hbm, grad_inputs),
    )
    for index, (source, target) in enumerate(sources):
        loads[index] = pltpu.make_async_copy(source, target, load_sem.at[index])
        loads[index].start()

    def store(source, target):
        copy = pltpu.make_async_copy(source, target, store_sem.at[len(stores)])
        copy.start()
        stores.append(copy)

    loads[0].wait()
    for row_tap in range(3):
        for tap in range(3):
            lanes = slice(tap * group, (tap + 1) * group)
            low = packed_mid[row_tap, :group, lanes].astype(F32)
            high = packed_mid[row_tap, group:, lanes].astype(F32)
            kernel_mid[row_tap, tap] = join_lanes(low, high, width)[:width, :real]
        store(kernel_mid.at[row_tap], kernel_mid_hbm.at[row_tap])
    loads[1].wait()
    for piece in range(4):
        kernel_out[piece * width : (piece + 1) * width, :] = packed_out[
            piece * group : piece * group + width, :real
        ].astype(F32)
    store(kernel_out, kernel_out_hbm)
    loads[2].wait()
    for side in range(2):
        rows = min(half, plan.channels - side * half)
        low = packed_in[side, :rows, :group].astype(F32)
        high = packed_in[side, :rows, group:].astype(F32)
        kernel_in[side * half : side * half + rows, :] = join_lanes(low, high, width)[:, :real]
    store(kernel_in, kernel_in_hbm)

    def maps(value, glob, small):
        def glob_row(row, carry):
            rows = pl.ds(pl.multiple_of(row * plan.glob_width, 16), plan.glob_width)
            glob[row, :, 0, :] = value(rows)[: plan.glob_side, : plan.channels]
            return carry

        def small_row(row, carry):
            place = plan.glob_own + row * plan.small_width
            rows = pl.ds(pl.multiple_of(place, 16), plan.small_width)
            small[row] = value(rows)[: plan.small_side, : plan.channels]
            return carry

        lax.fori_loop(0, plan.glob_height, glob_row, 0)
        lax.fori_loop(0, plan.slots * plan.small_height, small_row, 0)

    loads[3].wait()
    def joined(array, rows):
        return join_lanes(array[0, rows, :].astype(F32), array[1, rows, :].astype(F32), real)

    maps(lambda rows: joined(result, rows), glob_out, small_out)
    store(glob_out, glob_out_hbm)
    store(small_out, small_out_hbm)
    loads[4].wait()
    loads[5].wait()
    maps(
        lambda rows: joined(grad_summed, rows)
        + jnp.concatenate([grad_inputs[0, rows, :], grad_inputs[1, rows, :]], 1).astype(F32),
        glob_grad,
        small_grad,
    )
    store(glob_grad, glob_grad_hbm)
    store(small_grad, small_grad_hbm)
    squeeze_out[:width, :] = squeeze[:width, :width]
    squeeze_out[width:, :] = squeeze[group : group + width, :width]
    excite_out[...] = join_lanes(excite[:, :group], excite[:, group:], width)[:width, :real]
    for copy in stores:
        copy.wait()


def finish(plan, result, grad_summed, grad_inputs, gathered_out, gathered_in, gathered_mid, excite, squeeze):
    shape = jax.ShapeDtypeStruct
    width, real, channels = plan.width, plan.half_real, plan.channels
    glob = (plan.glob_height, plan.glob_side, 1, channels)
    small = (plan.slots * plan.small_height, plan.small_side, channels)
    outs = (glob, small, glob, small, (channels, real), (3, 3, width, real), (channels, real))
    ins = (gathered_mid, gathered_out, gathered_in, result, grad_summed, grad_inputs)
    loaded = (result, grad_summed, grad_inputs, gathered_out, gathered_in, gathered_mid)
    return pl.pallas_call(
        functools.partial(finish_kernel, plan),
        out_shape=tuple(shape(out, F32) for out in outs)
        + (shape((real, width), F32), shape((width, real), F32)),
        in_specs=[ANY] * 6 + [VMEM] * 2,
        out_specs=(ANY,) * 7 + (VMEM,) * 2,
        scratch_shapes=[pltpu.VMEM(array.shape, BF16) for array in loaded]
        + [pltpu.VMEM(out, F32) for out in outs]
        + [pltpu.SemaphoreType.DMA((6,)), pltpu.SemaphoreType.DMA((9,))],
        compiler_params=pltpu.CompilerParams(vmem_limit_bytes=VMEM_BYTES),
    )(result, grad_summed, grad_inputs, gathered_out, gathered_in, gathered_mid, excite, squeeze)


def ungroup_lanes(array, plan):
    return jnp.concatenate(
        [array[..., : plan.width], array[..., plan.group : plan.group + plan.width]], -1
    )


def per_device(
    glob_in,
    small_in,
    small_count,
    kernel_in,
    kernel_mid,
    kernel_out,
    squeeze_weight,
    squeeze_bias,
    excite_weight,
    excite_bias,
    gain_first,
    shift_first,
    gain_second,
    shift_second,
    gain_third,
    shift_third,
    glob_cotangent,
    small_cotangent,
):
    plan = Plan(glob_in.shape, small_in.shape, kernel_mid.shape[2], lax.axis_size("dp"))
    core = lax.axis_index("rows")
    width, real = plan.width, plan.half_real

    def images(maps):
        return maps.reshape((-1,) + maps.shape[2:])

    glob, small = images(glob_in), images(small_in)
    vec_raw = vector_table(
        [gain_first, shift_first, gain_second, shift_second, excite_bias, squeeze_bias, None, None]
        + [gain_third, shift_third]
        + [None] * 6,
        plan,
    )
    (
        x_all, pre_one, act_one, pre_two, act_three, w_mid, k_out, w_in, vec_three_other, vec, mask,
        w_squeeze, w_excite, stats, pooled, excite, squeeze_pre
    ) = forward(
        plan, small_count, glob, small, kernel_in, images(kernel_mid), kernel_out, squeeze_weight,
        excite_weight, vec_raw
    )
    result, grad_summed, grad_pre_three, sums_three = third(
        plan, small_count, act_three, k_out, glob, small, images(glob_cotangent),
        images(small_cotangent), vec, vec_raw, vec_three_other
    )
    shard_out, grad_norm, grad_excite, grad_squeeze, sums_two = second(
        plan, grad_pre_three, act_three, k_out, pre_two, stats, vec, mask, pooled, excite,
        squeeze_pre, w_squeeze, w_excite
    )
    gathered_out, gathered_mid, gathered_in, grad_inputs, sums_one = first(
        plan, shard_out, grad_norm, pre_two, pre_one, act_one, x_all, w_mid, w_in, stats, vec,
        sums_two, mask
    )
    (
        glob_out, small_out, glob_grad, small_grad, grad_kernel_in, grad_kernel_mid,
        grad_kernel_out, grad_squeeze, grad_excite
    ) = finish(
        plan, result, grad_summed, grad_inputs, gathered_out, gathered_in, gathered_mid,
        grad_excite, grad_squeeze
    )
    sums = lax.dynamic_index_in_dim(sums_three, core, 0, False)

    def grouped(row):
        return ungroup_lanes(row, plan)

    return (
        glob_out.reshape(glob_in.shape),
        small_out.reshape(small_in.shape),
        glob_grad.reshape(glob_in.shape),
        small_grad.reshape(small_in.shape),
        grad_kernel_in,
        grad_kernel_mid,
        grad_kernel_out,
        grad_squeeze,
        sums_two[SQUEEZE_SUM, :width],
        grad_excite,
        grouped(sums_two[EXCITE_SUM]),
        grouped(sums_one[GAIN_ONE_SUM]),
        grouped(sums_one[SHIFT_ONE_SUM]),
        grouped(sums_two[GAIN_TWO_SUM]),
        grouped(sums_two[SHIFT_TWO_SUM]),
        sums[1, :real],
        sums[0, :real],
    )


def solution(mesh):
    maps = P("dp", "rows", None, None)
    vector = P("rows")
    columns = P(None, "rows")
    taps = P(None, None, None, "rows")
    return jax.shard_map(
        per_device,
        mesh=mesh,
        in_specs=(
            maps, maps, P("dp"), columns, taps, columns, P("rows", None), P(), columns,
        )
        + (vector,) * 7
        + (maps, maps),
        out_specs=(maps,) * 4
        + (columns, taps, columns, P("rows", None), P(), columns)
        + (vector,) * 7,
        check_vma=False,
    )
```

profile of v0, /device:TPU:1, one launch (start us, length us, event | category | flops | bytes accessed | tf_op | source)
XLA Modules:
  0.0 371.1 jit_solution(8992645684571577208)
XLA Ops:
  0.7 5.6 %concatenate.22 = f32[12288]{0:T(1024)S(1)} concatenate(bf16[746]{0:T(1024)(128)(2,1)} %param.28, f32[22]{0:T(128)S(1)} %broadcast.6, bf16[746]{0:T(1024)(128)(2,1)} %param.29, f32[22]{0:T(128)S(1)} %broadcast.6, bf16[746]{0:T(1024)(128)(2,1)} %param.30, f32[22]{0:T(128)S(1)} %broadcast.6, bf16[746]{0:T(1024)(128)(2,1)} %param.31, f32[22]{0:T(128)S(1)} %broadcast.6, ...), dimensions={0} | concatenate | bytes 87114 | tf_op jit(solution)/shard_map/concatenate | solution.py:648
  6.3 0.6 reshape.77.vec_raw
  7.5 63.8 %shard_map.305 = (bf16[2,1856,768]{2,1,0:T(8,128)(2,1)}, f32[1856,768]{1,0:T(8,128)}, bf16[2000,768]{1,0:T(8,128)(2,1)}, f32[2000,768]{1,0:T(8,128)}, bf16[2,185...) custom-call(s32[1]{0:T(128)S(6)} %copy.35.live, ...), custom_call_target="tpu_custom_call" | custom-call | tf_op jit(solution)/shard_map/pallas_call | solution.py:580
  71.4 42.8 %shard_map.306 = (bf16[2,928,768]{2,1,0:T(8,128)(2,1)}, bf16[2,928,768]{2,1,0:T(8,128)(2,1)}, bf16[2,1856,768]{2,1,0:T(8,128)(2,1)}, f32[2,8,768]{2,1,0:T(8,128)}) custom-call(s32[1]{0:T(128)S(6)} %copy.35.live, bf16[2,1856,768]{2,1,0:T(8,128)(2,1)} %get-tuple-element.57.act_three_hbm, bf16[2,2,768,768]{3,2,1,0:T(8,128)(2,1)} %get-tuple-element.58.k_out_hbm, ...), custom_call_target="tpu_custom_call" | custom-call | tf_op jit(solution)/shard_map/pallas_call | solution.py:915
  114.2 47.2 %shard_map.307 = (bf16[384,768]{1,0:T(8,128)(2,1)}, f32[1856,768]{1,0:T(8,128)}, f32[384,768]{1,0:T(8,128)}, f32[768,384]{1,0:T(8,128)}, f32[8,768]{1,0:T(8,128)}) custom-call(bf16[2,1856,768]{2,1,0:T(8,128)(2,1)} %get-tuple-element.63.grad_pre_three_hbm, bf16[2,1856,768]{2,1,0:T(8,128)(2,1)} %get-tuple-element.57.act_three_hbm, ...), custom_call_target="tpu_custom_call" | custom-call | tf_op jit(solution)/shard_map/pallas_call | solution.py:1289
  161.4 1.5 slice_reduce_fusion.3
  162.9 0.7 pad_maximum_fusion.4
  163.5 183.1 %shard_map.308 = (bf16[1536,768]{1,0:T(8,128)(2,1)}, bf16[3,768,1152]{2,1,0:T(8,128)(2,1)}, bf16[2,768,768]{2,1,0:T(8,128)(2,1)}, bf16[2,928,768]{2,1,0:T(8,128)(2,1)}, f32[8,768]{1,0:T(8,128)}) custom-call(bf16[384,768]{1,0:T(8,128)(2,1)} %get-tuple-element.72.shard_out_hbm, f32[1856,768]{1,0:T(8,128)} %get-tuple-element.73.grad_norm_hbm, ...), custom_call_target="tpu_custom_call" | custom-call | tf_op jit(solution)/shard_map/pallas_call | solution.py:1613
  346.6 0.8 slice_reduce_fusion.7
  347.4 0.7 pad_maximum_fusion.1
  348.1 0.7 pad_maximum_fusion
  348.8 0.0 copy-start
  348.8 21.4 %shard_map.309 = (f32[14,28,1,1492]{3,2,1,0:T(1,128)}, f32[30,12,1492]{2,1,0:T(8,128)}, f32[14,28,1,1492]{3,2,1,0:T(1,128)}, f32[30,12,1492]{2,1,0:T(8,128)}, f3...) custom-call(bf16[2,928,768]{2,1,0:T(8,128)(2,1)} %get-tuple-element., ...), custom_call_target="tpu_custom_call" | custom-call | tf_op jit(solution)/shard_map/pallas_call | solution.py:1790
  370.2 0.0 copy-done
  370.2 0.6 slice_reduce_fusion
  (5 shorter events, 0.0 us)
Async XLA Ops:
  348.8 21.4 %copy-start = (f32[2,8,768]{2,1,0:T(8,128)S(1)}, f32[2,8,768]{2,1,0:T(8,128)}, u32[]{:S(2)}) copy-start(f32[2,8,768]{2,1,0:T(8,128)} %get-tuple-element.96) | copy-start | bytes 147460
where the time goes:
time: 377 us; the launch traced here: 371 us
  Pallas kernels  358 us (95%)
  local copies, waits for them, and re-layouts  9.12 us (2%)
    pallas_call x1, Pallas kernels, first(): pl.pallas_call(functools.partial(first_kernel, plan), out_shape=(shape((2...  183 us
    pallas_call x1, Pallas kernels, forward(): pl.pallas_call(functools.partial(forward_kernel, plan), out_shape=(shape(...  63.8 us
    pallas_call x1, Pallas kernels, second(): pl.pallas_call(functools.partial(second_kernel, plan), out_shape=(shape((...  47.2 us
    pallas_call x1, Pallas kernels, third(): pl.pallas_call(functools.partial(third_kernel, plan), out_shape=(shape(ow...  42.8 us
    pallas_call x1, Pallas kernels, finish(): pl.pallas_call(functools.partial(finish_kernel, plan), out_shape=tuple((s...  21.4 us

commit v1 on v0

--- a/solution.py
+++ b/solution.py
@@ -272,7 +272,14 @@
     kernel_out_hbm,
     squeeze_hbm,
     excite_hbm,
-    vec_raw,
+    gain_one,
+    shift_one,
+    gain_two,
+    shift_two,
+    excite_bias,
+    squeeze_bias,
+    gain_three,
+    shift_three,
     x_out,
     pre_one_out,
     act_one_out,
@@ -281,6 +288,7 @@
     w_mid_out,
     k_out_both,
     w_in_both,
+    vec_three,
     vec_three_other,
     vec,
     mask,
@@ -391,12 +399,20 @@
     send_in = partner(w_in, w_in_both.at[core], base)
 
     live_count = live[0].astype(F32)
-    raw = vec_raw[:8, :]
+    vec[...] = jnp.zeros_like(vec)
+    for index, vector in enumerate(
+        (gain_one, shift_one, gain_two, shift_two, excite_bias, squeeze_bias)
+    ):
+        vec[index : index + 1, : vector.shape[0]] = vector[...].astype(F32).reshape(1, -1)
+    vec_three[...] = jnp.zeros_like(vec_three)
+    for index, vector in enumerate((gain_three, shift_three)):
+        vec_three[index : index + 1, : vector.shape[0]] = vector[...].astype(F32).reshape(1, -1)
+    raw = vec[...]
     grouped = group_lanes(raw, plan)
     chip_count = jnp.zeros((1, half), F32) + (plan.glob_area + plan.slot_area * live_count)
     row = row_of(raw.shape)
     vec[...] = jnp.where(row == SQUEEZE_BIAS, raw, jnp.where(row == COUNT, chip_count, grouped))
-    send_vec = partner(vec_raw.at[pl.ds(8, 8), :], vec_three_other, base + 1)
+    send_vec = partner(vec_three, vec_three_other, base + 1)
     fill_mask(plan, mask, plan.glob_all, plan.slot_all, live_count)
 
     def product(owner):
@@ -570,7 +586,7 @@
 
 
 def forward(
-    plan, live, glob, small, kernel_in, kernel_mid, kernel_out, squeeze, excite, vec_raw
+    plan, live, glob, small, kernel_in, kernel_mid, kernel_out, squeeze, excite, vectors
 ):
     n, half, group = plan.dp, plan.half, plan.group
     shape = jax.ShapeDtypeStruct
@@ -590,6 +606,7 @@
             shape((2, 2, half, half), BF16),
             shape((8, half), F32),
             shape((8, half), F32),
+            shape((8, half), F32),
             shape((plan.all, LANE), F32),
             shape((half, group), BF16),
             shape((group, half), BF16),
@@ -598,8 +615,8 @@
             shape((plan.slot_rows, half), F32),
             shape((plan.slot_rows, group), F32),
         ),
-        in_specs=[smem] + [ANY] * 7 + [VMEM],
-        out_specs=(ANY,) * 8 + (VMEM,) * 9,
+        in_specs=[smem] + [ANY] * 7 + [VMEM] * 8,
+        out_specs=(ANY,) * 8 + (VMEM,) * 10,
         scratch_shapes=[
             pltpu.VMEM(glob.shape, BF16),
             pltpu.VMEM(small.shape, BF16),
@@ -633,19 +650,7 @@
         compiler_params=pltpu.CompilerParams(
             collective_id=0, has_side_effects=True, vmem_limit_bytes=VMEM_BYTES
         ),
-    )(live, glob, small, kernel_in, kernel_mid, kernel_out, squeeze, excite, vec_raw)
-
-
-def vector_table(vectors, plan):
-    pieces = []
-    for vector in vectors:
-        size = 0
-        if vector is not None:
-            size = vector.shape[0]
-            pieces.append(vector.astype(F32))
-        if plan.half > size:
-            pieces.append(jnp.zeros((plan.half - size,), F32))
-    return jnp.concatenate(pieces).reshape(len(vectors), plan.half)
+    )(live, glob, small, kernel_in, kernel_mid, kernel_out, squeeze, excite, *vectors)
 
 
 def own_steps(plan, body, carry):
@@ -671,13 +676,13 @@
     return total, spread, count
 
 
-def split_maps(plan, glob, small, target, wide):
+def split_maps(plan, glob, small, target, base, wide):
     half, real = plan.half, plan.half_real
     low = real // LANE * LANE
 
     def place(source, row, start, size, real_size):
         wide[:real_size, : plan.channels] = source[row].astype(F32)
-        rows = pl.ds(pl.multiple_of(start, 16), size)
+        rows = pl.ds(pl.multiple_of(base + start, 16), size)
         first = wide[:size, :half]
         target[0, rows, :] = jnp.where(lane_of(first.shape) < real, first, 0.0).astype(BF16)
         second = wide[:size, low:]
@@ -699,264 +704,11 @@
     lax.fori_loop(0, plan.slots * plan.small_height, small_row, 0)
 
 
-def third_kernel(
-    plan,
-    live,
-    act_three_hbm,
-    k_out_hbm,
-    glob_hbm,
-    small_hbm,
-    glob_cot_hbm,
-    small_cot_hbm,
-    vec,
-    vec_raw,
-    vec_three_other,
-    result_out,
-    grad_summed_out,
-    grad_pre_three_out,
-    sums_out,
-    act_three,
-    k_out,
-    pre_three,
-    grad_summed,
-    grad_pre_three,
-    pay,
-    pair,
-    chip,
-    slots,
-    finals,
-    pay_back,
-    pair_back,
-    chip_back,
-    slots_back,
-    finals_back,
-    vec_three,
-    glob,
-    small,
-    glob_cot,
-    small_cot,
-    x_own,
-    cot_own,
-    mask,
-    wide,
-    local_sem,
-    send_sem,
-    recv_sem,
-    spread_send,
-    spread_recv,
-):
-    n, half = plan.dp, plan.half
-    me, core = lax.axis_index("dp"), lax.axis_index("rows")
-    pieces = plan.own_pieces(core)
-
-    def local(source, target, index):
-        copy = pltpu.make_async_copy(source, target, local_sem.at[index])
-        copy.start()
-        return copy
-
-    def partner(source, target, index):
-        copy = to_partner(me, core, source, target, send_sem.at[index], recv_sem.at[index])
-        copy.start()
-        return copy
-
-    loads = [
-        local(
-            act_three_hbm.at[:, pl.ds(place, length), :],
-            act_three.at[:, pl.ds(start, length), :],
-            index,
-        )
-        for index, (place, start, length) in enumerate(pieces)
-    ]
-    base = len(pieces)
-    loads.append(local(k_out_hbm, k_out, base))
-    raws = [
-        local(source, target, 3 * base + 1 + index)
-        for index, (source, target) in enumerate(
-            (
-                (glob_hbm, glob),
-                (small_hbm, small),
-                (glob_cot_hbm, glob_cot),
-                (small_cot_hbm, small_cot),
-            )
-        )
-    ]
-    entry_barrier(n, me, core)
-    vec_three[core] = vec_raw[8:, :]
-    vec_three[1 - core] = vec_three_other[...]
-    fill_mask(plan, mask, plan.glob_own, plan.slot_own, live[0].astype(F32))
-    for copy in loads:
-        copy.wait()
-    own_count = 0.5 * vec[COUNT : COUNT + 1, :]
-
-    block = plan.own // 2
-    for side in range(2):
-
-        def product(part, carry, side=side):
-            rows = pl.ds(pl.multiple_of(part * block, 16), block)
-            pre_three[side, rows, :] = dot(act_three[0, rows, :], k_out[side, 0]) + dot(
-                act_three[1, rows, :], k_out[side, 1]
-            )
-            return carry
-
-        lax.fori_loop(0, 2, product, 0)
-
-    for side in range(2):
-
-        def add(row, step, carry, side=side):
-            rows = pl.ds(row, step)
-            return carry + rows_down(pre_three[side, rows, :] * widen(mask[rows, :], half))
-
-        total = jnp.sum(own_steps(plan, add, jnp.zeros((8, half), F32)), 0, keepdims=True)
-        mean = total / own_count
-
-        def spread(row, step, carry, side=side, mean=mean):
-            rows = pl.ds(row, step)
-            gap = (pre_three[side, rows, :] - mean) * widen(mask[rows, :], half)
-            return carry + rows_down(gap * gap)
-
-        squares = jnp.sum(own_steps(plan, spread, jnp.zeros((8, half), F32)), 0, keepdims=True)
-        pay[side, :, :half] = total
-        pay[side, :, half : 2 * half] = squares
-        pay[side, :, 2 * half :] = own_count[:, :LANE]
-    partner(pay.at[1 - core], pair, 0).wait()
-    total, squares, count = merge_two(pay[core], pair[...], half)
-    chip[:, :half] = total
-    chip[:, half : 2 * half] = squares
-    chip[:, 2 * half :] = count[:, :LANE]
-    exchange = Spread(n, me, core, chip, slots, spread_send.at[0], spread_recv.at[0])
-    exchange.start()
-    for copy in raws:
-        copy.wait()
-    split_maps(plan, glob, small, x_own, wide)
-    split_maps(plan, glob_cot, small_cot, cot_own, wide)
-    exchange.wait()
-    mean, variance, full_count = merge_moments(slots, n, half)
-    finals[core, :, :half] = mean
-    finals[core, :, half:] = lax.rsqrt(variance + EPSILON)
-    partner(finals.at[core], finals.at[core], 1).wait()
-
-    for side in range(2):
-        mean = finals[side, :, :half]
-        inverse = finals[side, :, half:]
-        gain = vec_three[side, :1, :]
-        shift = vec_three[side, 1:2, :]
-
-        def outer(row, step, carry, side=side, mean=mean, inverse=inverse, gain=gain, shift=shift):
-            rows = pl.ds(row, step)
-            seen = widen(mask[rows, :], half)
-            normed = (pre_three[side, rows, :] - mean) * inverse
-            summed = normed * gain + shift + x_own[side, rows, :].astype(F32)
-            sigma = sigmoid(summed)
-            result_out[side, rows, :] = (seen * summed * sigma).astype(BF16)
-            slope = sigma * (1.0 + summed * (1.0 - sigma))
-            grad = cot_own[side, rows, :].astype(F32) * seen * slope
-            grad_summed[side, rows, :] = grad
-            grad_summed_out[side, rows, :] = grad.astype(BF16)
-            return carry[0] + rows_down(grad), carry[1] + rows_down(grad * normed)
-
-        zero = jnp.zeros((8, half), F32)
-        shift_sum, gain_sum = own_steps(plan, outer, (zero, zero))
-        pay_back[side, :, :half] = jnp.sum(shift_sum, 0, keepdims=True)
-        pay_back[side, :, half:] = jnp.sum(gain_sum, 0, keepdims=True)
-    partner(pay_back.at[1 - core], pair_back, 2).wait()
-    chip_back[...] = pay_back[core] + pair_back[...]
-    exchange = Spread(n, me, core, chip_back, slots_back, spread_send.at[1], spread_recv.at[1])
-    exchange.start()
-    exchange.wait()
-
-    finals_back[core] = gather_sum(slots_back, n, 2 * half)
-    partner(finals_back.at[core], finals_back.at[core], 3).wait()
-    copies = []
-    for side in range(2):
-        mean = finals[side, :, :half]
-        inverse = finals[side, :, half:]
-        shift_sum = finals_back[side, :, :half]
-        gain_sum = finals_back[side, :, half:]
-        sums_out[side] = jnp.concatenate([shift_sum, gain_sum, jnp.zeros((6, half), F32)], 0)
-        scale = vec_three[side, :1, :] * inverse
-        shift_mean = shift_sum / full_count
-        gain_mean = gain_sum / full_count
-
-        def inner(
-            row, step, carry, side=side, mean=mean, inverse=inverse, scale=scale,
-            shift_mean=shift_mean, gain_mean=gain_mean
-        ):
-            rows = pl.ds(row, step)
-            normed = (pre_three[side, rows, :] - mean) * inverse
-            grad = scale * (grad_summed[side, rows, :] - shift_mean - normed * gain_mean)
-            grad_pre_three[side, rows, :] = (grad * widen(mask[rows, :], half)).astype(BF16)
-            return carry
-
-        own_steps(plan, inner, 0)
-        for index, (place, start, length) in enumerate(pieces):
-            source = grad_pre_three.at[side, pl.ds(start, length), :]
-            target = grad_pre_three_out.at[side, pl.ds(place, length), :]
-            copies.append(partner(source, target, 4 + side * base + index))
-            copies.append(local(source, target, base + 1 + side * base + index))
-    for copy in copies:
-        copy.wait()
-
-
 def gather_sum(slots, n, lanes):
     def add(step, carry):
         return carry + slots[step]
 
     return lax.fori_loop(0, n, add, jnp.zeros((1, lanes), F32))
-
-
-def third(
-    plan, live, act_three, k_out, glob, small, glob_cot, small_cot, vec, vec_raw, vec_three_other
-):
-    n, half = plan.dp, plan.half
-    shape = jax.ShapeDtypeStruct
-    pieces = 1 + plan.slots
-    pay = 2 * half + LANE
-    own = (2, plan.own, half)
-    return pl.pallas_call(
-        functools.partial(third_kernel, plan),
-        out_shape=(
-            shape(own, BF16),
-            shape(own, BF16),
-            shape((2, plan.all, half), BF16),
-            shape((2, 8, half), F32),
-        ),
-        in_specs=[pl.BlockSpec(memory_space=pltpu.SMEM)] + [ANY] * 6 + [VMEM] * 3,
-        out_specs=(VMEM, VMEM, ANY, VMEM),
-        scratch_shapes=[
-            pltpu.VMEM(own, BF16),
-            pltpu.VMEM(k_out.shape, BF16),
-            pltpu.VMEM(own, F32),
-            pltpu.VMEM(own, F32),
-            pltpu.VMEM(own, BF16),
-            pltpu.VMEM((2, 1, pay), F32),
-            pltpu.VMEM((1, pay), F32),
-            pltpu.VMEM((1, pay), F32),
-            pltpu.VMEM((n, 1, pay), F32),
-            pltpu.VMEM((2, 1, 2 * half), F32),
-            pltpu.VMEM((2, 1, 2 * half), F32),
-            pltpu.VMEM((1, 2 * half), F32),
-            pltpu.VMEM((1, 2 * half), F32),
-            pltpu.VMEM((n, 1, 2 * half), F32),
-            pltpu.VMEM((2, 1, 2 * half), F32),
-            pltpu.VMEM((2,) + vec_three_other.shape, F32),
-            pltpu.VMEM(glob.shape, BF16),
-            pltpu.VMEM(small.shape, BF16),
-            pltpu.VMEM(glob.shape, BF16),
-            pltpu.VMEM(small.shape, BF16),
-            pltpu.VMEM(own, BF16),
-            pltpu.VMEM(own, BF16),
-            pltpu.VMEM((plan.own, LANE), F32),
-            pltpu.VMEM((32, 2 * half), F32),
-            pltpu.SemaphoreType.DMA((3 * pieces + 5,)),
-            pltpu.SemaphoreType.DMA((2 * pieces + 4,)),
-            pltpu.SemaphoreType.DMA((2 * pieces + 4,)),
-            pltpu.SemaphoreType.DMA((2, n)),
-            pltpu.SemaphoreType.DMA((2, n)),
-        ],
-        compiler_params=pltpu.CompilerParams(
-            collective_id=1, has_side_effects=True, vmem_limit_bytes=VMEM_BYTES
-        ),
-    )(live, act_three, k_out, glob, small, glob_cot, small_cot, vec, vec_raw, vec_three_other)
 
 
 ORDERS = {
@@ -965,18 +717,19 @@
     "P": ((0, 1, 2, 3), (2, 1, 0, 3)),
     "Q": ((2, 0, 1, 3), (1, 0, 2, 3)),
 }
+HALVINGS = 3
 HANDED = 2
 
 
 class Steps:
     def __init__(self, n, me, core, order):
         bits = n.bit_length() - 1
-        self.halvings = min(bits, 4)
+        self.halvings = min(bits, HALVINGS)
         self.shards = 2**self.halvings
         self.doublings = bits - self.halvings
         self.bit, self.partner = [], []
         chosen = [[bit for bit in one if bit < bits] for one in ORDERS[order]]
-        chosen = [one + list(range(self.halvings, bits)) for one in chosen]
+        chosen = [one + list(range(len(one), bits)) for one in chosen]
         for step in range(bits):
             first, second = 2 ** chosen[0][step], 2 ** chosen[1][step]
             distance = first + (second - first) * core
@@ -1091,7 +844,7 @@
 
 def land_rows(n, rows, begun=0, until=None):
     bits = n.bit_length() - 1
-    halvings = min(bits, 4)
+    halvings = min(bits, HALVINGS)
     last = halvings if until is None else min(until, halvings)
     extra = bits - halvings if until is None else 0
     return (rows >> begun) - (rows >> last) + extra * (rows >> halvings)
@@ -1099,53 +852,89 @@
 
 def chain_slots(n):
     bits = n.bit_length() - 1
-    return bits + min(bits, 4)
+    return bits + min(bits, HALVINGS)
 
 
 def silu_slope(value, sigma):
     return sigma * (1.0 + value * (1.0 - sigma))
-SHIFT_TWO_SUM, GAIN_TWO_SUM, EXCITE_SUM, SQUEEZE_SUM = range(4)
+OUTS = 2
+MIDS = 6
+INS = 4
+CHAINS = (
+    tuple("out%d" % i for i in range(OUTS))
+    + tuple("mid%d" % i for i in range(MIDS))
+    + tuple("in%d" % i for i in range(INS))
+)
+CHAIN_ORDERS = tuple("AAPQAPQAPQPQ")
+
+SHIFT_TWO_SUM, GAIN_TWO_SUM = range(2)
 SHIFT_ONE_SUM, GAIN_ONE_SUM = range(2)
 
 
-def second_kernel(
+def middle_kernel(
     plan,
-    grad_pre_three_hbm,
+    live,
     act_three_hbm,
     k_out_hbm,
+    glob_hbm,
+    small_hbm,
+    glob_cot_hbm,
+    small_cot_hbm,
     pre_two_hbm,
     stats,
     vec,
+    vec_three_own,
+    vec_three_other,
     mask,
     pooled,
     excite,
     squeeze_pre,
     w_squeeze,
     w_excite,
+    result_out,
+    grad_summed_out,
     shard_out,
     grad_norm_out,
-    grad_excite_out,
-    grad_squeeze_out,
+    slots_ahead,
+    slots_behind,
+    sums_three_out,
     sums_out,
-    grad_pre_three,
     act_three,
     k_out,
+    flat,
+    flat_two,
+    maps,
+    pay,
+    pair,
+    chip,
+    slots,
+    finals,
+    pay_back,
+    pair_back,
+    chip_back,
+    slots_back,
+    finals_back,
+    vec_three,
+    glob,
+    small,
+    glob_cot,
+    small_cot,
+    mask_own,
+    wide,
     pre_two,
-    grad_act,
-    slopes,
     work,
     land,
     grad_excite,
     squeeze_send,
     squeeze_recv,
     grad_pooled,
-    factors,
-    factor_slots,
-    pay,
-    slots,
+    ahead,
+    behind,
+    pay_two,
+    slots_two,
     local_sem,
-    pair_send,
-    pair_recv,
+    send_sem,
+    recv_sem,
     spread_send,
     spread_recv,
     reduce_send,
@@ -1153,21 +942,201 @@
 ):
     n, half, group = plan.dp, plan.half, plan.group
     me, core = lax.axis_index("dp"), lax.axis_index("rows")
-    entry_barrier(n, me, core)
+    pieces = plan.own_pieces(core)
+    base = len(pieces)
 
     def local(source, target, index):
         copy = pltpu.make_async_copy(source, target, local_sem.at[index])
         copy.start()
         return copy
 
-    loads = [
-        local(grad_pre_three_hbm, grad_pre_three, 0),
-        local(act_three_hbm, act_three, 1),
-        local(k_out_hbm.at[:, core], k_out, 2),
-        local(pre_two_hbm, pre_two, 3),
+    def partner(source, target, index):
+        copy = to_partner(me, core, source, target, send_sem.at[index], recv_sem.at[index])
+        copy.start()
+        return copy
+
+    load_act = local(act_three_hbm, act_three, 0)
+    load_k = local(k_out_hbm, k_out, 1)
+    raws = [
+        local(source, target, 2 + index)
+        for index, (source, target) in enumerate(
+            (
+                (glob_hbm, glob),
+                (small_hbm, small),
+                (glob_cot_hbm, glob_cot),
+                (small_cot_hbm, small_cot),
+            )
+        )
     ]
-    loads[0].wait()
-    loads[1].wait()
+    load_two = local(pre_two_hbm, pre_two, 6)
+    entry_barrier(n, me, core)
+    vec_three[core] = vec_three_own[...]
+    vec_three[1 - core] = vec_three_other[...]
+    fill_mask(plan, mask_own, plan.glob_own, plan.slot_own, live[0].astype(F32))
+    own_count = 0.5 * vec[COUNT : COUNT + 1, :]
+    own = plan.own
+
+    def spread_of(source, target, index):
+        spread = Spread(n, me, core, source, target, spread_send.at[index], spread_recv.at[index])
+        spread.start()
+        return spread
+
+    deep = plan.slot_rows
+    before = squeeze_pre[...]
+    sigma = sigmoid(before)
+    squeezed = before * sigma
+    ahead[...] = jnp.zeros_like(ahead)
+    ahead[:deep, :] = pooled[...].astype(BF16)
+    ahead[deep:, :group] = squeezed.astype(BF16)
+    ahead_spread = spread_of(ahead, slots_ahead, 3)
+
+    def own_part(array, side, part):
+        if part == 0:
+            return array[side, pl.ds(pieces[0][0], plan.glob_own), :]
+        return jnp.concatenate(
+            [array[side, pl.ds(spot, size), :] for spot, _, size in pieces[1:]], 0
+        )
+
+    marks = (0, plan.glob_own, own)
+    load_act.wait()
+    load_k.wait()
+    for part in range(2):
+        lefts = [own_part(act_three, index, part) for index in range(2)]
+        for side in range(2):
+            flat[side * own + marks[part] : side * own + marks[part + 1], :] = dot(
+                lefts[0], k_out[side, 0]
+            ) + dot(lefts[1], k_out[side, 1])
+
+    for side in range(2):
+
+        def add(row, step, carry, side=side):
+            seen = widen(mask_own[pl.ds(row, step), :], half)
+            return carry + rows_down(flat[pl.ds(side * own + row, step), :] * seen)
+
+        total = jnp.sum(own_steps(plan, add, jnp.zeros((8, half), F32)), 0, keepdims=True)
+        mean = total / own_count
+
+        def spread_out(row, step, carry, side=side, mean=mean):
+            seen = widen(mask_own[pl.ds(row, step), :], half)
+            gap = (flat[pl.ds(side * own + row, step), :] - mean) * seen
+            return carry + rows_down(gap * gap)
+
+        squares = jnp.sum(own_steps(plan, spread_out, jnp.zeros((8, half), F32)), 0, keepdims=True)
+        pay[side, :, :half] = total
+        pay[side, :, half : 2 * half] = squares
+        pay[side, :, 2 * half :] = own_count[:, :LANE]
+    partner(pay.at[1 - core], pair, 0).wait()
+    total, squares, count = merge_two(pay[core], pair[...], half)
+    chip[:, :half] = total
+    chip[:, half : 2 * half] = squares
+    chip[:, 2 * half :] = count[:, :LANE]
+    exchange = spread_of(chip, slots, 0)
+    for copy in raws:
+        copy.wait()
+    split_maps(plan, glob, small, maps, 0, wide)
+    split_maps(plan, glob_cot, small_cot, maps, own, wide)
+    exchange.wait()
+    mean, variance, full_count = merge_moments(slots, n, half)
+    finals[core, :, :half] = mean
+    finals[core, :, half:] = lax.rsqrt(variance + EPSILON)
+    partner(finals.at[core], finals.at[core], 1).wait()
+
+    for side in range(2):
+        mean = finals[side, :, :half]
+        inverse = finals[side, :, half:]
+        gain = vec_three[side, :1, :]
+        shift = vec_three[side, 1:2, :]
+
+        def outer(row, step, carry, side=side, mean=mean, inverse=inverse, gain=gain, shift=shift):
+            rows = pl.ds(row, step)
+            low = pl.ds(side * own + row, step)
+            seen = widen(mask_own[rows, :], half)
+            normed = (flat[low, :] - mean) * inverse
+            summed = normed * gain + shift + maps[side, rows, :].astype(F32)
+            sigma = sigmoid(summed)
+            result_out[side, rows, :] = (seen * summed * sigma).astype(BF16)
+            slope = sigma * (1.0 + summed * (1.0 - sigma))
+            cot = maps[side, pl.ds(pl.multiple_of(own + row, 16), step), :]
+            grad = cot.astype(F32) * seen * slope
+            flat_two[low, :] = grad
+            grad_summed_out[side, rows, :] = grad.astype(BF16)
+            return carry[0] + rows_down(grad), carry[1] + rows_down(grad * normed)
+
+        zero = jnp.zeros((8, half), F32)
+        shift_sum, gain_sum = own_steps(plan, outer, (zero, zero))
+        pay_back[side, :, :half] = jnp.sum(shift_sum, 0, keepdims=True)
+        pay_back[side, :, half:] = jnp.sum(gain_sum, 0, keepdims=True)
+    partner(pay_back.at[1 - core], pair_back, 2).wait()
+    chip_back[...] = pay_back[core] + pair_back[...]
+    spread_of(chip_back, slots_back, 1).wait()
+    finals_back[core] = gather_sum(slots_back, n, 2 * half)
+    partner(finals_back.at[core], finals_back.at[core], 3).wait()
+
+    grad_pre_three = maps
+    swaps = []
+    for side in range(2):
+        mean = finals[side, :, :half]
+        inverse = finals[side, :, half:]
+        shift_sum = finals_back[side, :, :half]
+        gain_sum = finals_back[side, :, half:]
+        sums_three_out[side] = jnp.concatenate([shift_sum, gain_sum, jnp.zeros((6, half), F32)], 0)
+        scale = vec_three[side, :1, :] * inverse
+        shift_mean = shift_sum / full_count
+        gain_mean = gain_sum / full_count * inverse
+
+        def inner(
+            place, row, side=side, mean=mean, scale=scale, shift_mean=shift_mean,
+            gain_mean=gain_mean
+        ):
+            step = 32
+            low = pl.ds(side * own + row, step)
+            seen = widen(mask_own[pl.ds(row, step), :], half)
+            centered = flat[low, :] - mean
+            grad = scale * (flat_two[low, :] - shift_mean - centered * gain_mean)
+            grad_pre_three[side, pl.ds(pl.multiple_of(place, 16), step), :] = (grad * seen).astype(
+                BF16
+            )
+
+        def glob_step(tile, carry):
+            row = pl.multiple_of(tile * 32, 32)
+            inner(pieces[0][0] + row, row)
+            return carry
+
+        def slot_step(tile, carry):
+            row = pl.multiple_of(plan.glob_own + tile * 32, 32)
+            slot = tile // (plan.slot_own // 32)
+            inner(pieces[1][0] + tile * 32 + slot * plan.slot_own, row)
+            return carry
+
+        lax.fori_loop(0, plan.glob_own // 32, glob_step, 0)
+        lax.fori_loop(0, plan.slots * plan.slot_own // 32, slot_step, 0)
+        for index, (place, _, length) in enumerate(pieces):
+            part = grad_pre_three.at[side, pl.ds(place, length), :]
+            swaps.append(partner(part, part, 5 + side * base + index))
+
+    grad_act = flat
+
+    def product(owner):
+        spots = plan.own_pieces(owner)
+        rows = pl.ds(spots[0][0], plan.glob_own)
+        grad_act[rows, :] = dot_nt(grad_pre_three[0, rows, :], k_out[0, core]) + dot_nt(
+            grad_pre_three[1, rows, :], k_out[1, core]
+        )
+        sides = [
+            jnp.concatenate(
+                [grad_pre_three[side, pl.ds(spot, size), :] for spot, _, size in spots[1:]], 0
+            )
+            for side in range(2)
+        ]
+        result = dot_nt(sides[0], k_out[0, core]) + dot_nt(sides[1], k_out[1, core])
+        for spot, start, size in spots[1:]:
+            low = start - plan.glob_own
+            grad_act[pl.ds(spot, size), :] = result[low : low + size]
+
+    product(core)
+    for swap in swaps:
+        swap.wait()
+    chains, size = [], 2 * half // OUTS
     for side in range(2):
         for part in range(2):
             lanes = slice(part * group, (part + 1) * group)
@@ -1175,29 +1144,23 @@
             work[low : low + group, :] = dot_tn(
                 act_three[side, :, lanes], grad_pre_three[core]
             ).astype(BF16)
-    reduction = Chain(
-        Steps(n, me, core, ORDER_OUT), work, land, reduce_send, reduce_recv, None, until=HANDED
-    )
-    reduction.advance()
-    loads[2].wait()
-
-    block = plan.all // 4
-
-    def product(part, carry):
-        rows = pl.ds(pl.multiple_of(part * block, 16), block)
-        grad_act[rows, :] = dot_nt(grad_pre_three[0, rows, :], k_out[0]) + dot_nt(
-            grad_pre_three[1, rows, :], k_out[1]
-        )
-        return carry
-
-    lax.fori_loop(0, 4, product, 0)
-    loads[3].wait()
+            if (low + group) % size == 0:
+                index = low // size
+                chain = Chain(
+                    Steps(n, me, core, CHAIN_ORDERS[index]), work.at[pl.ds(index * size, size), :],
+                    land.at[index], reduce_send.at[index], reduce_recv.at[index], None, until=HANDED
+                )
+                chain.advance()
+                chains.append(chain)
+    product(1 - core)
+    load_two.wait()
 
     mean = stats[MEAN_TWO : MEAN_TWO + 1, :]
     inverse = stats[INVERSE_TWO : INVERSE_TWO + 1, :]
     count = stats[TOTAL : TOTAL + 1, :]
     gain = vec[GAIN_TWO : GAIN_TWO + 1, :]
     shift = vec[SHIFT_TWO : SHIFT_TWO + 1, :]
+    slopes = flat_two
     grad_excite[...] = jnp.zeros_like(grad_excite)
 
     def excitation(start, place, crop, carry):
@@ -1215,25 +1178,16 @@
     grad_excite_pre = grad_excite[...] * level * (1.0 - level)
     part = split_dot(grad_excite_pre, w_excite[...], nt=True)
     squeeze_send[...] = part
-    swap = to_partner(me, core, squeeze_send, squeeze_recv, pair_send.at[0], pair_recv.at[0])
-    swap.start()
-    reduction.advance()
+    swap = partner(squeeze_send, squeeze_recv, 4)
     swap.wait()
-    before = squeeze_pre[...]
-    sigma = sigmoid(before)
-    squeezed = before * sigma
     grad_squeeze_pre = (part + squeeze_recv[...]) * silu_slope(before, sigma)
     back = split_dot(grad_squeeze_pre, w_squeeze[...], nt=True)
     crop_row = lax.broadcasted_iota(jnp.int32, back.shape, 0)
     area = jnp.where(crop_row == 0, 1.0 / plan.glob_area, 1.0 / plan.slot_area)
     grad_pooled[...] = back * area
-    deep = plan.slot_rows
-    factors[:deep, :group] = squeezed.astype(BF16)
-    factors[:deep, group:] = grad_excite_pre.astype(BF16)
-    factors[deep:, :group] = grad_squeeze_pre.astype(BF16)
-    factors[deep:, group:] = pooled[...].astype(BF16)
-    factor_spread = Spread(n, me, core, factors, factor_slots, spread_send.at[0], spread_recv.at[0])
-    factor_spread.start()
+    behind[...] = jnp.zeros_like(behind)
+    behind[:deep, :] = grad_excite_pre.astype(BF16)
+    behind[deep:, :group] = grad_squeeze_pre.astype(BF16)
 
     def gradient(start, place, crop, carry):
         rows = pl.ds(start, TILE)
@@ -1245,102 +1199,115 @@
 
     zero = jnp.zeros((8, half), F32)
     shift_sum, gain_sum = plan.sweep(gradient, (zero, zero))
-    save = local(grad_act, grad_norm_out, 4)
-    pay[:, :half] = jnp.sum(shift_sum, 0, keepdims=True)
-    pay[:, half:] = jnp.sum(gain_sum, 0, keepdims=True)
-    spread = Spread(n, me, core, pay, slots, spread_send.at[1], spread_recv.at[1])
-    spread.start()
-    while not reduction.done():
-        reduction.advance()
-    store = local(reduction.here(), shard_out, 5)
-    factor_spread.wait()
-    left = factor_slots[:, :, :group].reshape(n * 2 * deep, group)
-    right = factor_slots[:, :, group:].reshape(n * 2 * deep, half)
-    upper = lax.broadcasted_iota(jnp.int32, left.shape, 0) % (2 * deep) < deep
-    zeros = jnp.zeros_like(left)
-    excite_left = jnp.where(upper, left, zeros)
-    squeeze_left = jnp.where(upper, zeros, left)
-    grad_excite_out[...] = dot_tn(excite_left, right)
-    grad_squeeze_out[...] = dot_tn(right, squeeze_left)
-    wide_upper = lax.broadcasted_iota(jnp.int32, right.shape, 0) % (2 * deep) < deep
-    excite_bias = jnp.sum(jnp.where(wide_upper, right.astype(F32), 0.0), 0, keepdims=True)
-    squeeze_bias = jnp.sum(squeeze_left.astype(F32), 0, keepdims=True)
+    save = local(grad_act, grad_norm_out, 7)
+    pay_two[:, :half] = jnp.sum(shift_sum, 0, keepdims=True)
+    pay_two[:, half:] = jnp.sum(gain_sum, 0, keepdims=True)
+    spread = spread_of(pay_two, slots_two, 2)
+    behind_spread = spread_of(behind, slots_behind, 4)
+    for chain in chains:
+        chain.advance()
+    ahead_spread.wait()
     spread.wait()
-    totals = gather_sum(slots, n, 2 * half)
+    totals = gather_sum(slots_two, n, 2 * half)
+    stores = []
+    for index, chain in enumerate(chains):
+        while not chain.done():
+            chain.advance()
+        stores.append(local(chain.here(), shard_out.at[index], 8 + index))
     sums_out[...] = jnp.zeros_like(sums_out)
     sums_out[SHIFT_TWO_SUM : SHIFT_TWO_SUM + 1, :] = totals[:, :half]
     sums_out[GAIN_TWO_SUM : GAIN_TWO_SUM + 1, :] = totals[:, half:]
-    sums_out[EXCITE_SUM : EXCITE_SUM + 1, :] = excite_bias
-    sums_out[SQUEEZE_SUM : SQUEEZE_SUM + 1, :group] = squeeze_bias
-    save.wait()
-    store.wait()
-
-
-def second(
-    plan, grad_pre_three, act_three, k_out, pre_two, stats, vec, mask, pooled, excite,
-    squeeze_pre, w_squeeze, w_excite
+    behind_spread.wait()
+    for copy in [save] + stores:
+        copy.wait()
+
+
+def middle(
+    plan, live, act_three, k_out, glob, small, glob_cot, small_cot, pre_two, stats, vec, vec_three,
+    vec_three_other, mask, pooled, excite, squeeze_pre, w_squeeze, w_excite
 ):
     n, half, group = plan.dp, plan.half, plan.group
     shape = jax.ShapeDtypeStruct
+    pieces = 1 + plan.slots
+    pay = 2 * half + LANE
+    own = (2, plan.own, half)
     rows = 2 * half
-    shard = rows >> HANDED
     deep = plan.slot_rows
-    bits = n.bit_length() - 1
     return pl.pallas_call(
-        functools.partial(second_kernel, plan),
+        functools.partial(middle_kernel, plan),
         out_shape=(
-            shape((shard, half), BF16),
+            shape(own, BF16),
+            shape(own, BF16),
+            shape((OUTS, rows // OUTS >> HANDED, half), BF16),
             shape((plan.all, half), F32),
-            shape((group, half), F32),
-            shape((half, group), F32),
+            shape((n, 2 * deep, half), BF16),
+            shape((n, 2 * deep, half), BF16),
+            shape((2, 8, half), F32),
             shape((8, half), F32),
         ),
-        in_specs=[ANY] * 4 + [VMEM] * 8,
-        out_specs=(ANY, ANY, VMEM, VMEM, VMEM),
+        in_specs=[pl.BlockSpec(memory_space=pltpu.SMEM)] + [ANY] * 7 + [VMEM] * 10,
+        out_specs=(VMEM, VMEM, ANY, ANY, VMEM, VMEM, VMEM, VMEM),
         scratch_shapes=[
             pltpu.VMEM((2, plan.all, half), BF16),
-            pltpu.VMEM((2, plan.all, half), BF16),
-            pltpu.VMEM((2, half, half), BF16),
-            pltpu.VMEM((plan.conv, half), F32),
+            pltpu.VMEM(k_out.shape, BF16),
             pltpu.VMEM((plan.all, half), F32),
             pltpu.VMEM((plan.all, half), F32),
+            pltpu.VMEM((2, plan.all, half), BF16),
+            pltpu.VMEM((2, 1, pay), F32),
+            pltpu.VMEM((1, pay), F32),
+            pltpu.VMEM((1, pay), F32),
+            pltpu.VMEM((n, 1, pay), F32),
+            pltpu.VMEM((2, 1, 2 * half), F32),
+            pltpu.VMEM((2, 1, 2 * half), F32),
+            pltpu.VMEM((1, 2 * half), F32),
+            pltpu.VMEM((1, 2 * half), F32),
+            pltpu.VMEM((n, 1, 2 * half), F32),
+            pltpu.VMEM((2, 1, 2 * half), F32),
+            pltpu.VMEM((2,) + vec_three.shape, F32),
+            pltpu.VMEM(glob.shape, BF16),
+            pltpu.VMEM(small.shape, BF16),
+            pltpu.VMEM(glob.shape, BF16),
+            pltpu.VMEM(small.shape, BF16),
+            pltpu.VMEM((plan.own, LANE), F32),
+            pltpu.VMEM((32, 2 * half), F32),
+            pltpu.VMEM((plan.conv, half), F32),
             pltpu.VMEM((rows, half), BF16),
-            pltpu.VMEM((land_rows(n, rows, until=HANDED), half), BF16),
+            pltpu.VMEM((OUTS, land_rows(n, rows // OUTS, until=HANDED), half), BF16),
             pltpu.VMEM((deep, half), F32),
             pltpu.VMEM((deep, group), F32),
             pltpu.VMEM((deep, group), F32),
             pltpu.VMEM((deep, half), F32),
-            pltpu.VMEM((2 * deep, group + half), BF16),
-            pltpu.VMEM((n, 2 * deep, group + half), BF16),
+            pltpu.VMEM((2 * deep, half), BF16),
+            pltpu.VMEM((2 * deep, half), BF16),
             pltpu.VMEM((1, 2 * half), F32),
             pltpu.VMEM((n, 1, 2 * half), F32),
-            pltpu.SemaphoreType.DMA((6,)),
-            pltpu.SemaphoreType.DMA((1,)),
-            pltpu.SemaphoreType.DMA((1,)),
-            pltpu.SemaphoreType.DMA((2, n)),
-            pltpu.SemaphoreType.DMA((2, n)),
-            pltpu.SemaphoreType.DMA((bits,)),
-            pltpu.SemaphoreType.DMA((bits,)),
+            pltpu.SemaphoreType.DMA((8 + OUTS,)),
+            pltpu.SemaphoreType.DMA((2 * pieces + 5,)),
+            pltpu.SemaphoreType.DMA((2 * pieces + 5,)),
+            pltpu.SemaphoreType.DMA((5, n)),
+            pltpu.SemaphoreType.DMA((5, n)),
+            pltpu.SemaphoreType.DMA((OUTS, HANDED)),
+            pltpu.SemaphoreType.DMA((OUTS, HANDED)),
         ],
         compiler_params=pltpu.CompilerParams(
-            collective_id=2, has_side_effects=True, vmem_limit_bytes=VMEM_BYTES
+            collective_id=1, has_side_effects=True, vmem_limit_bytes=VMEM_BYTES
         ),
     )(
-        grad_pre_three, act_three, k_out, pre_two, stats, vec, mask, pooled, excite, squeeze_pre,
-        w_squeeze, w_excite
+        live, act_three, k_out, glob, small, glob_cot, small_cot, pre_two, stats, vec, vec_three,
+        vec_three_other, mask, pooled, excite, squeeze_pre, w_squeeze, w_excite
     )
 
 
-CHAINS = ("out", "mid0", "mid1", "mid2", "in0", "in1")
-ORDER_OUT = "A"
-CHAIN_ORDERS = (ORDER_OUT, "B", "P", "Q", "P", "Q")
 SCHEDULE = (
-    "two", "M0", "M1", "C0", "out", "C1", "C2", "C3", "C4", "C5", "mid0", "out", "mid1", "C6",
-    "C7", "sums", "out", "M2", "mid1", "out", "one", "K0", "mid2", "mid0", "mid1", "K1",
-    "mid1", "mid2", "in0", "mid0", "mid1", "mid0", "X0", "X1", "in1", "in0", "mid2", "mid0",
-    "out", "mid1", "mid2", "in1", "mid2", "X2", "mid0", "in0", "in0", "mid2", "mid1", "in1",
-    "in0", "in1", "mid2", "in1", "in1", "in0", "mid0", "mid1", "X3", "in1", "in0", "mid2",
-    "out", "mid0", "in0", "in1",
+    "two", "M0", "M1", "C0", "out1", "M2", "M3", "M4", "mid0", "M5", "mid2", "out0", "C1",
+    "C2", "mid3", "C3", "out1", "mid1", "mid4", "mid2", "C4", "out0", "C5", "out1", "mid0",
+    "mid2", "C6", "out0", "C7", "mid1", "mid2", "mid5", "mid0", "sums", "mid4", "out1",
+    "mid3", "mid5", "mid2", "mid0", "mid1", "mid4", "one", "K0", "K1", "K2", "mid2", "K3",
+    "mid3", "in0", "X0", "in1", "X1", "mid5", "mid4", "in2", "mid1", "in3", "in1", "mid3",
+    "mid0", "in0", "mid4", "mid5", "in3", "in2", "X2", "in0", "out0", "mid1", "in1", "mid0",
+    "mid5", "in3", "mid3", "X3", "in2", "mid2", "in1", "mid4", "in3", "in0", "in2", "mid1",
+    "in1", "in3", "in2", "mid0", "mid3", "mid4", "out1", "in0", "in3", "mid5", "in0", "in2",
+    "in1", "mid3", "mid1", "mid5", "in0", "in3", "out0", "in1", "in2",
 )
 
 
@@ -1417,15 +1384,22 @@
             index = CHAINS.index(name)
             saves[name] = local(chain.work, targets[name], 8 + index)
 
-    out = begin("out", work_out, land_out, gathered_out, HANDED)
-    load_shard = local(shard_out_hbm, out.here(), 2)
+    outs = CHAINS[:OUTS]
+    loads = []
+    for index, name in enumerate(outs):
+        rows = pl.ds(index * (2 * half // OUTS), 2 * half // OUTS)
+        out = begin(
+            name, work_out.at[rows, :], land_out.at[index], gathered_out.at[rows, :], HANDED
+        )
+        loads.append(local(shard_out_hbm.at[index], out.here(), 8 + index))
     waits["norm"] = local(grad_norm_hbm, flat, 0)
     waits["two"] = local(pre_two_hbm, conv_rows, 1)
     waits["act"] = local(act_one_hbm, act_one, 3)
     waits["mid"] = local(w_mid_hbm, w_mid, 4)
     waits["in"] = local(w_in_hbm, w_in, 5)
-    load_shard.wait()
-    advance("out")
+    for name, load in zip(outs, loads):
+        load.wait()
+        advance(name)
     count = stats[TOTAL : TOTAL + 1, :]
 
     def norm_two():
@@ -1456,8 +1430,10 @@
         waits["one"] = local(pre_one_hbm, flat, 0)
         waits["act"].wait()
 
-    def mid(tap):
-        for side in range(2):
+    def mid(index):
+        tap = index * 3 // MIDS
+        sides = range(2) if MIDS == 3 else (index % 2,)
+        for side in sides:
             lanes = slice(side * group, (side + 1) * group)
             total = None
             for low, length, width in plan.segments():
@@ -1467,14 +1443,15 @@
                 )
                 total = term if total is None else total + term
             work_mid[tap, lanes, :] = total.astype(BF16)
-        name = CHAINS[1 + tap]
-        begin(name, work_mid.at[tap], land_mid.at[tap], gathered_mid.at[tap])
+        name = CHAINS[OUTS + index]
+        rows = pl.ds(sides[0] * group, len(sides) * group)
+        begin(name, work_mid.at[tap, rows, :], land_mid.at[index], gathered_mid.at[tap, rows, :])
         advance(name)
         read_shifted()
 
     def read_shifted():
         state["reads"] = state.get("reads", 0) + 1
-        if state["reads"] == 3 + 8:
+        if state["reads"] == MIDS + 8:
             waits["x"] = local(x_hbm, shifted.at[:, pl.ds(0, plan.all), pl.ds(0, half)], 7)
 
     def conv(index):
@@ -1551,16 +1528,18 @@
             swap.start()
             state["swaps"].append(swap)
 
-    def kernel_in(side):
-        if side == 0:
+    def kernel_in(index):
+        if index == 0:
             waits["x"].wait()
-        for part in range(2):
-            lanes = slice(part * group, (part + 1) * group)
-            work_in[side, lanes, :] = dot_tn(
-                shifted[side, : plan.all, lanes], grad_pre_one[...]
+        size = 2 * half // INS
+        side, start = index * size // half, index * size % half
+        for low in range(start, start + size, group):
+            work_in[side, low : low + group, :] = dot_tn(
+                shifted[side, : plan.all, low : low + group], grad_pre_one[...]
             ).astype(BF16)
-        name = CHAINS[4 + side]
-        begin(name, work_in.at[side], land_in.at[side], gathered_in.at[side])
+        name = CHAINS[OUTS + MIDS + index]
+        rows = pl.ds(start, size)
+        begin(name, work_in.at[side, rows, :], land_in.at[index], gathered_in.at[side, rows, :])
         advance(name)
 
     def inputs(index):
@@ -1574,21 +1553,28 @@
         pieces = plan.own_pieces(core)
         pieces = pieces[:1] if part == 0 else pieces[1:]
         own = jnp.concatenate([grad_pre_one[pl.ds(spot, size), :] for spot, _, size in pieces], 0)
-        grad_inputs_out[side, rows, :] = (
+        low = side * plan.own + marks[part]
+        act_one[low : low + own.shape[0], :] = (
             dot_nt(own, w_in[core, side]) + dot_nt(grad_other[rows, :], w_in[1 - core, side])
         ).astype(BF16)
+        if part == 1:
+            waits["result%d" % side] = local(
+                act_one.at[pl.ds(side * plan.own, plan.own), :],
+                grad_inputs_out.at[side],
+                8 + len(CHAINS) + side,
+            )
 
     blocks = {
         "two": norm_two,
         "sums": sums_one,
         "one": norm_one,
     }
-    for tap in range(3):
-        blocks["M%d" % tap] = functools.partial(mid, tap)
+    for index in range(MIDS):
+        blocks["M%d" % index] = functools.partial(mid, index)
     for index in range(8):
         blocks["C%d" % index] = functools.partial(conv, index)
-    for side in range(2):
-        blocks["K%d" % side] = functools.partial(kernel_in, side)
+    for index in range(INS):
+        blocks["K%d" % index] = functools.partial(kernel_in, index)
     for index in range(4):
         blocks["X%d" % index] = functools.partial(inputs, index)
     for item in SCHEDULE:
@@ -1601,6 +1587,8 @@
             advance(name)
     for name in CHAINS:
         saves[name].wait()
+    for side in range(2):
+        waits["result%d" % side].wait()
 
 
 def first(
@@ -1620,7 +1608,7 @@
             shape((8, half), F32),
         ),
         in_specs=[ANY] * 8 + [VMEM] * 4,
-        out_specs=(ANY, ANY, ANY, VMEM, VMEM),
+        out_specs=(ANY, ANY, ANY, ANY, VMEM),
         scratch_shapes=[
             pltpu.VMEM((plan.all, half), F32),
             pltpu.VMEM((plan.conv, half), F32),
@@ -1631,24 +1619,24 @@
             pltpu.VMEM((plan.own, half), BF16),
             pltpu.VMEM(w_in.shape, BF16),
             pltpu.VMEM((2 * half, half), BF16),
-            pltpu.VMEM((land_rows(n, 2 * half, begun=HANDED), half), BF16),
+            pltpu.VMEM((OUTS, land_rows(n, 2 * half // OUTS, begun=HANDED), half), BF16),
             pltpu.VMEM((3, half, 3 * group), BF16),
-            pltpu.VMEM((3, land_rows(n, half), 3 * group), BF16),
+            pltpu.VMEM((MIDS, land_rows(n, 3 * half // MIDS), 3 * group), BF16),
             pltpu.VMEM((2, half, half), BF16),
-            pltpu.VMEM((2, land_rows(n, half), half), BF16),
+            pltpu.VMEM((INS, land_rows(n, 2 * half // INS), half), BF16),
             pltpu.VMEM((1, 2 * half), F32),
             pltpu.VMEM((n, 1, 2 * half), F32),
-            pltpu.SemaphoreType.DMA((14,)),
+            pltpu.SemaphoreType.DMA((10 + len(CHAINS),)),
             pltpu.SemaphoreType.DMA((pieces,)),
             pltpu.SemaphoreType.DMA((pieces,)),
             pltpu.SemaphoreType.DMA((n,)),
             pltpu.SemaphoreType.DMA((n,)),
             pltpu.SemaphoreType.DMA((len(CHAINS), chain_slots(n))),
             pltpu.SemaphoreType.DMA((len(CHAINS), chain_slots(n))),
-            pltpu.SemaphoreType.REGULAR((len(CHAINS), 4)),
+            pltpu.SemaphoreType.REGULAR((len(CHAINS), HALVINGS)),
         ],
         compiler_params=pltpu.CompilerParams(
-            collective_id=3, has_side_effects=True, vmem_limit_bytes=VMEM_BYTES
+            collective_id=2, has_side_effects=True, vmem_limit_bytes=VMEM_BYTES
         ),
     )(
         shard_out, grad_norm, pre_two, pre_one, act_one, x_all, w_mid, w_in, stats, vec, sums_two,
@@ -1672,8 +1660,11 @@
     out_hbm,
     in_hbm,
     mid_hbm,
-    excite,
-    squeeze,
+    slots_ahead,
+    slots_behind,
+    sums_one,
+    sums_two,
+    sums_three,
     glob_out_hbm,
     small_out_hbm,
     glob_grad_hbm,
@@ -1682,7 +1673,15 @@
     kernel_mid_hbm,
     kernel_out_hbm,
     squeeze_out,
+    squeeze_bias,
     excite_out,
+    excite_bias,
+    gain_one,
+    shift_one,
+    gain_two,
+    shift_two,
+    gain_three,
+    shift_three,
     result,
     grad_summed,
     grad_inputs,
@@ -1772,14 +1771,40 @@
     )
     store(glob_grad, glob_grad_hbm)
     store(small_grad, small_grad_hbm)
+    n, deep = plan.dp, plan.slot_rows
+
+    def crops(slots, low, lanes):
+        rows = slots[...].astype(F32)[:, low : low + deep, :lanes]
+        return rows.reshape(n * deep, lanes)
+
+    wide_pooled, squeezed = crops(slots_ahead, 0, half), crops(slots_ahead, deep, group)
+    grad_excite, grad_squeeze = crops(slots_behind, 0, half), crops(slots_behind, deep, group)
+    excite = dot_tn(squeezed.astype(BF16), grad_excite.astype(BF16))
+    squeeze = dot_tn(wide_pooled.astype(BF16), grad_squeeze.astype(BF16))
     squeeze_out[:width, :] = squeeze[:width, :width]
     squeeze_out[width:, :] = squeeze[group : group + width, :width]
     excite_out[...] = join_lanes(excite[:, :group], excite[:, group:], width)[:width, :real]
+    bias = jnp.sum(grad_excite, 0, keepdims=True)
+    bias = join_lanes(bias[:, :group], bias[:, group:], width)
+    two = join_lanes(sums_two[:, :group], sums_two[:, group:], width)
+    one = join_lanes(sums_one[:, :group], sums_one[:, group:], width)
+    three = sums_three[lax.axis_index("rows")]
+    squeeze_bias[...] = jnp.sum(grad_squeeze, 0)[:width]
+    excite_bias[...] = bias[0, :real]
+    gain_one[...] = one[GAIN_ONE_SUM, :real]
+    shift_one[...] = one[SHIFT_ONE_SUM, :real]
+    gain_two[...] = two[GAIN_TWO_SUM, :real]
+    shift_two[...] = two[SHIFT_TWO_SUM, :real]
+    gain_three[...] = three[1, :real]
+    shift_three[...] = three[0, :real]
     for copy in stores:
         copy.wait()
 
 
-def finish(plan, result, grad_summed, grad_inputs, gathered_out, gathered_in, gathered_mid, excite, squeeze):
+def finish(
+    plan, result, grad_summed, grad_inputs, gathered_out, gathered_in, gathered_mid, slots_ahead,
+    slots_behind, sums_one, sums_two, sums_three
+):
     shape = jax.ShapeDtypeStruct
     width, real, channels = plan.width, plan.half_real, plan.channels
     glob = (plan.glob_height, plan.glob_side, 1, channels)
@@ -1790,19 +1815,17 @@
     return pl.pallas_call(
         functools.partial(finish_kernel, plan),
         out_shape=tuple(shape(out, F32) for out in outs)
-        + (shape((real, width), F32), shape((width, real), F32)),
-        in_specs=[ANY] * 6 + [VMEM] * 2,
-        out_specs=(ANY,) * 7 + (VMEM,) * 2,
+        + (shape((real, width), F32), shape((width,), F32), shape((width, real), F32))
+        + (shape((real,), F32),) * 7,
+        in_specs=[ANY] * 6 + [VMEM] * 5,
+        out_specs=(ANY,) * 7 + (VMEM,) * 10,
         scratch_shapes=[pltpu.VMEM(array.shape, BF16) for array in loaded]
         + [pltpu.VMEM(out, F32) for out in outs]
         + [pltpu.SemaphoreType.DMA((6,)), pltpu.SemaphoreType.DMA((9,))],
         compiler_params=pltpu.CompilerParams(vmem_limit_bytes=VMEM_BYTES),
-    )(result, grad_summed, grad_inputs, gathered_out, gathered_in, gathered_mid, excite, squeeze)
-
-
-def ungroup_lanes(array, plan):
-    return jnp.concatenate(
-        [array[..., : plan.width], array[..., plan.group : plan.group + plan.width]], -1
+    )(
+        result, grad_summed, grad_inputs, gathered_out, gathered_in, gathered_mid, slots_ahead,
+        slots_behind, sums_one, sums_two, sums_three
     )
 
 
@@ -1827,69 +1850,39 @@
     small_cotangent,
 ):
     plan = Plan(glob_in.shape, small_in.shape, kernel_mid.shape[2], lax.axis_size("dp"))
-    core = lax.axis_index("rows")
-    width, real = plan.width, plan.half_real
 
     def images(maps):
         return maps.reshape((-1,) + maps.shape[2:])
 
     glob, small = images(glob_in), images(small_in)
-    vec_raw = vector_table(
-        [gain_first, shift_first, gain_second, shift_second, excite_bias, squeeze_bias, None, None]
-        + [gain_third, shift_third]
-        + [None] * 6,
-        plan,
+    vectors = (
+        gain_first, shift_first, gain_second, shift_second, excite_bias, squeeze_bias, gain_third,
+        shift_third
     )
     (
-        x_all, pre_one, act_one, pre_two, act_three, w_mid, k_out, w_in, vec_three_other, vec, mask,
-        w_squeeze, w_excite, stats, pooled, excite, squeeze_pre
+        x_all, pre_one, act_one, pre_two, act_three, w_mid, k_out, w_in, vec_three,
+        vec_three_other, vec, mask, w_squeeze, w_excite, stats, pooled, excite, squeeze_pre
     ) = forward(
         plan, small_count, glob, small, kernel_in, images(kernel_mid), kernel_out, squeeze_weight,
-        excite_weight, vec_raw
+        excite_weight, vectors
     )
-    result, grad_summed, grad_pre_three, sums_three = third(
+    (
+        result, grad_summed, shard_out, grad_norm, slots_ahead, slots_behind, sums_three, sums_two
+    ) = middle(
         plan, small_count, act_three, k_out, glob, small, images(glob_cotangent),
-        images(small_cotangent), vec, vec_raw, vec_three_other
-    )
-    shard_out, grad_norm, grad_excite, grad_squeeze, sums_two = second(
-        plan, grad_pre_three, act_three, k_out, pre_two, stats, vec, mask, pooled, excite,
-        squeeze_pre, w_squeeze, w_excite
+        images(small_cotangent), pre_two, stats, vec, vec_three, vec_three_other, mask, pooled,
+        excite, squeeze_pre, w_squeeze, w_excite
     )
     gathered_out, gathered_mid, gathered_in, grad_inputs, sums_one = first(
         plan, shard_out, grad_norm, pre_two, pre_one, act_one, x_all, w_mid, w_in, stats, vec,
         sums_two, mask
     )
-    (
-        glob_out, small_out, glob_grad, small_grad, grad_kernel_in, grad_kernel_mid,
-        grad_kernel_out, grad_squeeze, grad_excite
-    ) = finish(
+    outputs = finish(
         plan, result, grad_summed, grad_inputs, gathered_out, gathered_in, gathered_mid,
-        grad_excite, grad_squeeze
+        slots_ahead, slots_behind, sums_one, sums_two, sums_three
     )
-    sums = lax.dynamic_index_in_dim(sums_three, core, 0, False)
-
-    def grouped(row):
-        return ungroup_lanes(row, plan)
-
-    return (
-        glob_out.reshape(glob_in.shape),
-        small_out.reshape(small_in.shape),
-        glob_grad.reshape(glob_in.shape),
-        small_grad.reshape(small_in.shape),
-        grad_kernel_in,
-        grad_kernel_mid,
-        grad_kernel_out,
-        grad_squeeze,
-        sums_two[SQUEEZE_SUM, :width],
-        grad_excite,
-        grouped(sums_two[EXCITE_SUM]),
-        grouped(sums_one[GAIN_ONE_SUM]),
-        grouped(sums_one[SHIFT_ONE_SUM]),
-        grouped(sums_two[GAIN_TWO_SUM]),
-        grouped(sums_two[SHIFT_TWO_SUM]),
-        sums[1, :real],
-        sums[0, :real],
-    )
+    shapes = (glob_in.shape, small_in.shape) * 2
+    return tuple(out.reshape(shape) for out, shape in zip(outputs, shapes)) + outputs[4:]
 
 
 def solution(mesh):

time: 377 us -> 317 us (0.84)
  the two profiles are of different devices: /device:TPU:1 before, /device:TPU:0 now
where the time goes in v1:
time: 317 us; the launch traced here: 311 us
  Pallas kernels  309 us (97%)
    pallas_call x1, Pallas kernels, first(): pl.pallas_call(functools.partial(first_kernel, plan), out_shape=(shape((2...  149 us
    pallas_call x1, Pallas kernels, middle(): pl.pallas_call(functools.partial(middle_kernel, plan), out_shape=(shape(o...  75 us
    pallas_call x1, Pallas kernels, forward(): pl.pallas_call(functools.partial(forward_kernel, plan), out_shape=(shape(...  64 us
    pallas_call x1, Pallas kernels, finish(): pl.pallas_call(functools.partial(finish_kernel, plan), out_shape=tuple((s...  21.4 us

profile of v1, /device:TPU:0, one launch (start us, length us, event | category | flops | bytes accessed | tf_op | source)
XLA Modules:
  0.0 311.0 jit_solution(14733078978859071688)
XLA Ops:
  1.3 64.0 %shard_map.305 = (bf16[2,1856,768]{2,1,0:T(8,128)(2,1)}, f32[1856,768]{1,0:T(8,128)}, bf16[2000,768]{1,0:T(8,128)(2,1)}, f32[2000,768]{1,0:T(8,128)}, bf16[2,185...) custom-call(s32[1]{0:T(128)S(6)} %copy.35.live, ...), custom_call_target="tpu_custom_call" | custom-call | tf_op jit(solution)/shard_map/pallas_call | solution.py:596
  65.3 75.0 %shard_map.306 = (bf16[2,928,768]{2,1,0:T(8,128)(2,1)}, bf16[2,928,768]{2,1,0:T(8,128)(2,1)}, bf16[2,192,768]{2,1,0:T(8,128)(2,1)}, f32[1856,768]{1,0:T(8,128)},...) custom-call(s32[1]{0:T(128)S(6)} %copy.35.live, ...), custom_call_target="tpu_custom_call" | custom-call | tf_op jit(solution)/shard_map/pallas_call | solution.py:1236
  140.3 149.0 %shard_map.307 = (bf16[1536,768]{1,0:T(8,128)(2,1)}, bf16[3,768,1152]{2,1,0:T(8,128)(2,1)}, bf16[2,768,768]{2,1,0:T(8,128)(2,1)}, bf16[2,928,768]{2,1,0:T(8,128)(2,1)}, f32[8,768]{1,0:T(8,128)}) custom-call(bf16[2,192,768]{2,1,0:T(8,128)(2,1)} %get-tuple-element.80.shard_out_hbm, f32[1856,768]{1,0:T(8,128)} %get-tuple-element.81.grad_norm_hbm, ...), custom_call_target="tpu_custom_call" | custom-call | tf_op jit(solution)/shard_map/pallas_call | solution.py:1601
  289.3 21.4 %shard_map.308 = (f32[14,28,1,1492]{3,2,1,0:T(1,128)}, f32[30,12,1492]{2,1,0:T(8,128)}, f32[14,28,1,1492]{3,2,1,0:T(1,128)}, f32[30,12,1492]{2,1,0:T(8,128)}, f3...) custom-call(bf16[2,928,768]{2,1,0:T(8,128)(2,1)} %get-tuple-element., ...), custom_call_target="tpu_custom_call" | custom-call | tf_op jit(solution)/shard_map/pallas_call | solution.py:1815
